TPU v7x, 512 devices: a whole 4x8x8 slice. The times are simulated.
512 devices in a mesh: gx: 16 (over z_hi, x, core), gy: 32 (over y, z_lo).
Axes of the slice: x: 4, y: 8, z: 8 (z_hi: 2, z_lo: 4; z = z_hi * 4 + z_lo), core: 2. Of those that a mesh axis runs over, the one named last changes fastest.
Arguments:
- start_vecs: float32 [16, 32, 4, 64, 128], P('gx', 'gy'), may hold values from -12 to 12
- force_blocks: bfloat16 [16, 32, 4, 27, 128, 128], P('gx', 'gy'), may hold values from -0.0625 to 0.0625
- slot_offsets: int32 [16, 32, 4, 27], P('gx', 'gy'), may hold values from 0 to 26, each once within a row
Outputs:
- moments: float32 [9, 32], replicated
- last_vecs: float32 [16, 32, 4, 64, 128], P('gx', 'gy')
Inputs may be any that keep to these rules, and one draw needn't show every extreme that they name: `slot_offsets`: each tile's 27 slots name the 27 offset codes once each.
All inputs are finite; a program needn't handle non-finite values.
Results may differ from a plain program's by a relative error of at most 0.0085.
Values may be sent and summed in bfloat16 or wider, within the bound.
A program may use at most 64 MiB of HBM per device.

v0:
```python
import jax
import jax.numpy as jnp
from jax import lax
from jax.sharding import PartitionSpec as P

STEPS = 8


def extended_2(cells, sides, width):
    for axis, dim in sides:
        count = lax.axis_size(axis)
        head = lax.slice_in_dim(cells, 0, width, axis=dim)
        tail = lax.slice_in_dim(cells, cells.shape[dim] - width, cells.shape[dim], axis=dim)
        cells = jnp.concatenate(
            [
                lax.ppermute(tail, axis, [(i, (i + 1) % count) for i in range(count)]),
                cells,
                lax.ppermute(head, axis, [((i + 1) % count, i) for i in range(count)]),
            ],
            axis=dim,
        )
    return cells


def offsets_of(code):
    return (code // 9 - 1, code // 3 % 3 - 1, code % 3 - 1)


def apply_operator(vec, ordered):
    rounded = vec.astype(jnp.bfloat16)
    span_x, span_y, depth = (rounded.shape[0], rounded.shape[1], rounded.shape[2])
    extended = extended_2(rounded, (("gx", 0), ("gy", 1)), 1)
    extended = jnp.pad(extended, ((0, 0), (0, 0), (1, 1), (0, 0), (0, 0)))
    pieces = []
    for code in range(27):
        step_x, step_y, step_z = offsets_of(code)
        pieces.append(
            extended[
                1 + step_x : 1 + step_x + span_x,
                1 + step_y : 1 + step_y + span_y,
                1 + step_z : 1 + step_z + depth,
            ]
        )
    stacked = jnp.stack(pieces, axis=3)
    return jnp.einsum("xyzocs,xyzors->xyzcr", stacked, ordered, preferred_element_type=jnp.float32)


def moment_of(first, current, half, rows_total):
    first_re, first_im = (first[:, :, :, :half], first[:, :, :, half:])
    cur_re, cur_im = (current[:, :, :, :half], current[:, :, :, half:])
    real_part = jnp.sum(first_re * cur_re + first_im * cur_im, axis=(0, 1, 2, 4))
    return real_part / rows_total


def summed_now(partial_moment):
    return lax.psum(partial_moment, ("gx", "gy"))


def body(start_vecs, force_blocks, slot_offsets):
    codes = lax.broadcasted_iota(jnp.int32, (1, 1, 1, 1, 27), 4)
    match = (slot_offsets[..., :, None] == codes).astype(jnp.bfloat16)
    ordered = jnp.einsum(
        "xyzkrs,xyzko->xyzors", force_blocks, match, preferred_element_type=jnp.float32
    ).astype(jnp.bfloat16)
    half = start_vecs.shape[3] // 2
    rows_total = float(
        lax.axis_size("gx") * lax.axis_size("gy") * start_vecs.shape[2] * start_vecs.shape[4]
    )
    previous = start_vecs
    current = apply_operator(start_vecs, ordered)
    partials = [
        moment_of(start_vecs, start_vecs, half, rows_total),
        moment_of(start_vecs, current, half, rows_total),
    ]
    for step in range(STEPS - 1):
        following = 2.0 * apply_operator(current, ordered) - previous
        previous, current = (current, following)
        partials.append(moment_of(start_vecs, current, half, rows_total))
    moments = jnp.stack([summed_now(part) for part in partials])
    return (moments, current)


def solution(mesh):
    in_specs = (
        P("gx", "gy", None, None, None),
        P("gx", "gy", None, None, None, None),
        P("gx", "gy", None, None),
    )
    out_specs = (P(), P("gx", "gy", None, None, None))
    return jax.shard_map(body, mesh=mesh, in_specs=in_specs, out_specs=out_specs, check_vma=False)
```

profile of v0, /device:TPU:1, one launch (start us, length us, event | category | flops | bytes accessed | tf_op | source)
XLA Modules:
  0.0 360.8 jit_solution(15669548669160704011)
XLA Ops:
  1.7 8.9 %collective-permute-start.1 = (bf16[1,1,4,64,128]{4,3,2,1,0:T(8,128)(2,1)S(1)}, bf16[1,1,4,64,128]{4,3,2,1,0:T(8,128)(2,1)S(1)}, u32[]{:S(2)}, u32[]{:S(2)}) collective-permute-start(bf16[1,1,4,64,128]{4,3,2,1,0:T(8,128)(2,1)S(1)} %convert_element_type.50), channel_id=1, source_target_pairs={{32,0},{64,32},{96,64},{128,96},{160,128},{192,160},{224,192},{256... | collective-permute-start | bytes 196616 | tf_op jit(solution)/shard_map/ppermute | solution.py:18
  12.6 6.0 %collective-permute-done = bf16[1,1,4,64,128]{4,3,2,1,0:T(8,128)(2,1)S(1)} collective-permute-done((bf16[1,1,4,64,128]{4,3,2,1,0:T(8,128)(2,1)S(1)}, bf16[1,1,4,64,128]{4,3,2,1,0:T(8,128)(2,1)S(1)}, u32[]{:S(2)}, u32[]{:S(2)}) %collective-permute-start) | collective-permute-done | bytes 65568 | tf_op jit(solution)/shard_map/ppermute | solution.py:16
  18.6 7.8 %collective-permute-start.3 = (bf16[3,1,4,64,128]{4,3,2,1,0:T(8,128)(2,1)S(1)}, bf16[3,1,4,64,128]{4,3,2,1,0:T(8,128)(2,1)S(1)}, u32[]{:S(2)}, u32[]{:S(2)}) collective-permute-start(bf16[3,1,4,64,128]{4,3,2,1,0:T(8,128)(2,1)S(1)} %pad_maximum_fusion), channel_id=1, source_target_pairs={{1,0},{2,1},{3,2},{4,3},{5,4},{6,5},{7,6},{8,7},{9,8},{10,9},{11,1... | collective-permute-start | bytes 589832 | tf_op jit(solution)/shard_map/ppermute | solution.py:18
  28.4 3.2 fusion
  31.6 5.3 %collective-permute-done.2 = bf16[3,1,4,64,128]{4,3,2,1,0:T(8,128)(2,1)S(1)} collective-permute-done((bf16[3,1,4,64,128]{4,3,2,1,0:T(8,128)(2,1)S(1)}, bf16[3,1,4,64,128]{4,3,2,1,0:T(8,128)(2,1)S(1)}, u32[]{:S(2)}, u32[]{:S(2)}) %collective-permute-start.2) | collective-permute-done | bytes 196640 | tf_op jit(solution)/shard_map/ppermute | solution.py:16
  38.9 12.8 %collective-permute-start.5 = (bf16[1,1,4,64,128]{4,3,2,1,0:T(8,128)(2,1)S(1)}, bf16[1,1,4,64,128]{4,3,2,1,0:T(8,128)(2,1)S(1)}, u32[]{:S(2)}, u32[]{:S(2)}) collective-permute-start(bf16[1,1,4,64,128]{4,3,2,1,0:T(8,128)(2,1)S(1)} %fusion.124), channel_id=1, source_target_pairs={{32,0},{64,32},{96,64},{128,96},{160,128},{192,160},{224,192},{256... | collective-permute-start | bytes 196616 | tf_op jit(solution)/shard_map/ppermute | solution.py:18
  56.9 3.4 collective-permute-start.6
  61.4 6.0 %collective-permute-done.6 = bf16[3,1,4,64,128]{4,3,2,1,0:T(8,128)(2,1)S(1)} collective-permute-done((bf16[3,1,4,64,128]{4,3,2,1,0:T(8,128)(2,1)S(1)}, bf16[3,1,4,64,128]{4,3,2,1,0:T(8,128)(2,1)S(1)}, u32[]{:S(2)}, u32[]{:S(2)}) %collective-permute-start.6) | collective-permute-done | bytes 196640 | tf_op jit(solution)/shard_map/ppermute | solution.py:16
  69.5 13.5 %collective-permute-start.9 = (bf16[1,1,4,64,128]{4,3,2,1,0:T(8,128)(2,1)S(1)}, bf16[1,1,4,64,128]{4,3,2,1,0:T(8,128)(2,1)S(1)}, u32[]{:S(2)}, u32[]{:S(2)}) collective-permute-start(bf16[1,1,4,64,128]{4,3,2,1,0:T(8,128)(2,1)S(1)} %get-tuple-element.20), channel_id=1, source_target_pairs={{32,0},{64,32},{96,64},{128,96},{160,128},{192,160},{224,192},{256... | collective-permute-start | bytes 196616 | tf_op jit(solution)/shard_map/ppermute | solution.py:18
  88.2 3.4 collective-permute-start.10
  93.0 5.7 %collective-permute-done.10 = bf16[3,1,4,64,128]{4,3,2,1,0:T(8,128)(2,1)S(1)} collective-permute-done((bf16[3,1,4,64,128]{4,3,2,1,0:T(8,128)(2,1)S(1)}, bf16[3,1,4,64,128]{4,3,2,1,0:T(8,128)(2,1)S(1)}, u32[]{:S(2)}, u32[]{:S(2)}) %collective-permute-start.10) | collective-permute-done | bytes 196640 | tf_op jit(solution)/shard_map/ppermute | solution.py:16
  100.7 11.9 %collective-permute-start.13 = (bf16[1,1,4,64,128]{4,3,2,1,0:T(8,128)(2,1)S(1)}, bf16[1,1,4,64,128]{4,3,2,1,0:T(8,128)(2,1)S(1)}, u32[]{:S(2)}, u32[]{:S(2)}) collective-permute-start(bf16[1,1,4,64,128]{4,3,2,1,0:T(8,128)(2,1)S(1)} %convert_bitcast_fusion.2), channel_id=1, source_target_pairs={{32,0},{64,32},{96,64},{128,96},{160,128},{192,160},{224,192},{256... | collective-permute-start | bytes 196616 | tf_op jit(solution)/shard_map/ppermute | solution.py:18
  116.0 1.9 collective-permute-start.15
  117.9 3.4 collective-permute-start.14
  122.7 5.7 %collective-permute-done.14 = bf16[3,1,4,64,128]{4,3,2,1,0:T(8,128)(2,1)S(1)} collective-permute-done((bf16[3,1,4,64,128]{4,3,2,1,0:T(8,128)(2,1)S(1)}, bf16[3,1,4,64,128]{4,3,2,1,0:T(8,128)(2,1)S(1)}, u32[]{:S(2)}, u32[]{:S(2)}) %collective-permute-start.14) | collective-permute-done | bytes 196640 | tf_op jit(solution)/shard_map/ppermute | solution.py:16
  130.4 13.0 %collective-permute-start.17 = (bf16[1,1,4,64,128]{4,3,2,1,0:T(8,128)(2,1)S(1)}, bf16[1,1,4,64,128]{4,3,2,1,0:T(8,128)(2,1)S(1)}, u32[]{:S(2)}, u32[]{:S(2)}) collective-permute-start(bf16[1,1,4,64,128]{4,3,2,1,0:T(8,128)(2,1)S(1)} %get-tuple-element.22), channel_id=1, source_target_pairs={{32,0},{64,32},{96,64},{128,96},{160,128},{192,160},{224,192},{256... | collective-permute-start | bytes 196616 | tf_op jit(solution)/shard_map/ppermute | solution.py:18
  148.6 3.5 collective-permute-start.18
  153.4 5.7 %collective-permute-done.18 = bf16[3,1,4,64,128]{4,3,2,1,0:T(8,128)(2,1)S(1)} collective-permute-done((bf16[3,1,4,64,128]{4,3,2,1,0:T(8,128)(2,1)S(1)}, bf16[3,1,4,64,128]{4,3,2,1,0:T(8,128)(2,1)S(1)}, u32[]{:S(2)}, u32[]{:S(2)}) %collective-permute-start.18) | collective-permute-done | bytes 196640 | tf_op jit(solution)/shard_map/ppermute | solution.py:16
  161.1 13.0 %collective-permute-start.21 = (bf16[1,1,4,64,128]{4,3,2,1,0:T(8,128)(2,1)S(1)}, bf16[1,1,4,64,128]{4,3,2,1,0:T(8,128)(2,1)S(1)}, u32[]{:S(2)}, u32[]{:S(2)}) collective-permute-start(bf16[1,1,4,64,128]{4,3,2,1,0:T(8,128)(2,1)S(1)} %convert_bitcast_fusion.1), channel_id=1, source_target_pairs={{32,0},{64,32},{96,64},{128,96},{160,128},{192,160},{224,192},{256... | collective-permute-start | bytes 196616 | tf_op jit(solution)/shard_map/ppermute | solution.py:18
  174.1 1.9 collective-permute-start.20
  177.4 1.9 collective-permute-start.23
  179.3 3.4 collective-permute-start.22
  184.1 5.7 %collective-permute-done.22 = bf16[3,1,4,64,128]{4,3,2,1,0:T(8,128)(2,1)S(1)} collective-permute-done((bf16[3,1,4,64,128]{4,3,2,1,0:T(8,128)(2,1)S(1)}, bf16[3,1,4,64,128]{4,3,2,1,0:T(8,128)(2,1)S(1)}, u32[]{:S(2)}, u32[]{:S(2)}) %collective-permute-start.22) | collective-permute-done | bytes 196640 | tf_op jit(solution)/shard_map/ppermute | solution.py:16
  191.8 13.0 %collective-permute-start.25 = (bf16[1,1,4,64,128]{4,3,2,1,0:T(8,128)(2,1)S(1)}, bf16[1,1,4,64,128]{4,3,2,1,0:T(8,128)(2,1)S(1)}, u32[]{:S(2)}, u32[]{:S(2)}) collective-permute-start(bf16[1,1,4,64,128]{4,3,2,1,0:T(8,128)(2,1)S(1)} %get-tuple-element.24), channel_id=1, source_target_pairs={{32,0},{64,32},{96,64},{128,96},{160,128},{192,160},{224,192},{256... | collective-permute-start | bytes 196616 | tf_op jit(solution)/shard_map/ppermute | solution.py:18
  204.8 1.9 collective-permute-start.24
  210.0 3.4 collective-permute-start.26
  214.8 5.7 %collective-permute-done.26 = bf16[3,1,4,64,128]{4,3,2,1,0:T(8,128)(2,1)S(1)} collective-permute-done((bf16[3,1,4,64,128]{4,3,2,1,0:T(8,128)(2,1)S(1)}, bf16[3,1,4,64,128]{4,3,2,1,0:T(8,128)(2,1)S(1)}, u32[]{:S(2)}, u32[]{:S(2)}) %collective-permute-start.26) | collective-permute-done | bytes 196640 | tf_op jit(solution)/shard_map/ppermute | solution.py:16
  222.5 13.0 %collective-permute-start.29 = (bf16[1,1,4,64,128]{4,3,2,1,0:T(8,128)(2,1)S(1)}, bf16[1,1,4,64,128]{4,3,2,1,0:T(8,128)(2,1)S(1)}, u32[]{:S(2)}, u32[]{:S(2)}) collective-permute-start(bf16[1,1,4,64,128]{4,3,2,1,0:T(8,128)(2,1)S(1)} %convert_bitcast_fusion), channel_id=1, source_target_pairs={{32,0},{64,32},{96,64},{128,96},{160,128},{192,160},{224,192},{256... | collective-permute-start | bytes 196616 | tf_op jit(solution)/shard_map/ppermute | solution.py:18
  240.7 3.4 collective-permute-start.30
  245.5 5.7 %collective-permute-done.30 = bf16[3,1,4,64,128]{4,3,2,1,0:T(8,128)(2,1)S(1)} collective-permute-done((bf16[3,1,4,64,128]{4,3,2,1,0:T(8,128)(2,1)S(1)}, bf16[3,1,4,64,128]{4,3,2,1,0:T(8,128)(2,1)S(1)}, u32[]{:S(2)}, u32[]{:S(2)}) %collective-permute-start.30) | collective-permute-done | bytes 196640 | tf_op jit(solution)/shard_map/ppermute | solution.py:16
  255.5 102.7 %all-reduce.8 = (f32[1,32]{1,0:T(1,128)}, f32[1,32]{1,0:T(1,128)}, f32[1,32]{1,0:T(1,128)}, f32[1,32]{1,0:T(1,128)}, f32[1,32]{1,0:T(1,128)}, /*index=5*/f32[1,3...) all-reduce(f32[1,32]{1,0:T(1,128)} %multiply_bitcast_fusion.8, ...), channel_id=1, replica_groups=mesh['gx'=16,'gy'=32] {'gx','gy'}, use_global_device_ids=true, to_apply=%region_1.2 | all-reduce | flops 288 | bytes 2304 | tf_op jit(solution)/shard_map/psum | solution.py:56
  358.2 2.6 stack.935
  (293 shorter events, 60.1 us)
Async XLA Ops:
  1.7 10.9 %collective-permute-start.1 = (bf16[1,1,4,64,128]{4,3,2,1,0:T(8,128)(2,1)S(1)}, bf16[1,1,4,64,128]{4,3,2,1,0:T(8,128)(2,1)S(1)}, u32[]{:S(2)}, u32[]{:S(2)}) collective-permute-start(bf16[1,1,4,64,128]{4,3,2,1,0:T(8,128)(2,1)S(1)} %convert_element_type.50), channel_id=1, source_target_pairs={{32,0},{64,32},{96,64},{128,96},{160,128},{192,160},{224,192},{256... | collective-permute-start | bytes 196616 | tf_op jit(solution)/shard_map/ppermute | solution.py:18
  10.6 7.9 %collective-permute-start = (bf16[1,1,4,64,128]{4,3,2,1,0:T(8,128)(2,1)S(1)}, bf16[1,1,4,64,128]{4,3,2,1,0:T(8,128)(2,1)S(1)}, u32[]{:S(2)}, u32[]{:S(2)}) collective-permute-start(bf16[1,1,4,64,128]{4,3,2,1,0:T(8,128)(2,1)S(1)} %convert_element_type.50), channel_id=1, source_target_pairs={{0,32},{32,64},{64,96},{96,128},{128,160},{160,192},{192,224},{224... | collective-permute-start | bytes 196616 | tf_op jit(solution)/shard_map/ppermute | solution.py:16
  18.6 13.0 %collective-permute-start.3 = (bf16[3,1,4,64,128]{4,3,2,1,0:T(8,128)(2,1)S(1)}, bf16[3,1,4,64,128]{4,3,2,1,0:T(8,128)(2,1)S(1)}, u32[]{:S(2)}, u32[]{:S(2)}) collective-permute-start(bf16[3,1,4,64,128]{4,3,2,1,0:T(8,128)(2,1)S(1)} %pad_maximum_fusion), channel_id=1, source_target_pairs={{1,0},{2,1},{3,2},{4,3},{5,4},{6,5},{7,6},{8,7},{9,8},{10,9},{11,1... | collective-permute-start | bytes 589832 | tf_op jit(solution)/shard_map/ppermute | solution.py:18
  26.4 10.5 %collective-permute-start.2 = (bf16[3,1,4,64,128]{4,3,2,1,0:T(8,128)(2,1)S(1)}, bf16[3,1,4,64,128]{4,3,2,1,0:T(8,128)(2,1)S(1)}, u32[]{:S(2)}, u32[]{:S(2)}) collective-permute-start(bf16[3,1,4,64,128]{4,3,2,1,0:T(8,128)(2,1)S(1)} %pad_maximum_fusion), channel_id=1, source_target_pairs={{0,1},{1,2},{2,3},{3,4},{4,5},{5,6},{6,7},{7,8},{8,9},{9,10},{10,1... | collective-permute-start | bytes 589832 | tf_op jit(solution)/shard_map/ppermute | solution.py:16
  38.9 14.7 %collective-permute-start.5 = (bf16[1,1,4,64,128]{4,3,2,1,0:T(8,128)(2,1)S(1)}, bf16[1,1,4,64,128]{4,3,2,1,0:T(8,128)(2,1)S(1)}, u32[]{:S(2)}, u32[]{:S(2)}) collective-permute-start(bf16[1,1,4,64,128]{4,3,2,1,0:T(8,128)(2,1)S(1)} %fusion.124), channel_id=1, source_target_pairs={{32,0},{64,32},{96,64},{128,96},{160,128},{192,160},{224,192},{256... | collective-permute-start | bytes 196616 | tf_op jit(solution)/shard_map/ppermute | solution.py:18
  51.7 3.2 collective-permute-start.4
  55.0 6.4 %collective-permute-start.7 = (bf16[3,1,4,64,128]{4,3,2,1,0:T(8,128)(2,1)S(1)}, bf16[3,1,4,64,128]{4,3,2,1,0:T(8,128)(2,1)S(1)}, u32[]{:S(2)}, u32[]{:S(2)}) collective-permute-start(bf16[3,1,4,64,128]{4,3,2,1,0:T(8,128)(2,1)S(1)} %pad_maximum_fusion.1), channel_id=1, source_target_pairs={{1,0},{2,1},{3,2},{4,3},{5,4},{6,5},{7,6},{8,7},{9,8},{10,9},{11,1... | collective-permute-start | bytes 589832 | tf_op jit(solution)/shard_map/ppermute | solution.py:18
  56.9 10.5 %collective-permute-start.6 = (bf16[3,1,4,64,128]{4,3,2,1,0:T(8,128)(2,1)S(1)}, bf16[3,1,4,64,128]{4,3,2,1,0:T(8,128)(2,1)S(1)}, u32[]{:S(2)}, u32[]{:S(2)}) collective-permute-start(bf16[3,1,4,64,128]{4,3,2,1,0:T(8,128)(2,1)S(1)} %pad_maximum_fusion.1), channel_id=1, source_target_pairs={{0,1},{1,2},{2,3},{3,4},{4,5},{5,6},{6,7},{7,8},{8,9},{9,10},{10,1... | collective-permute-start | bytes 589832 | tf_op jit(solution)/shard_map/ppermute | solution.py:16
  69.5 15.5 %collective-permute-start.9 = (bf16[1,1,4,64,128]{4,3,2,1,0:T(8,128)(2,1)S(1)}, bf16[1,1,4,64,128]{4,3,2,1,0:T(8,128)(2,1)S(1)}, u32[]{:S(2)}, u32[]{:S(2)}) collective-permute-start(bf16[1,1,4,64,128]{4,3,2,1,0:T(8,128)(2,1)S(1)} %get-tuple-element.20), channel_id=1, source_target_pairs={{32,0},{64,32},{96,64},{128,96},{160,128},{192,160},{224,192},{256... | collective-permute-start | bytes 196616 | tf_op jit(solution)/shard_map/ppermute | solution.py:18
  83.0 3.2 collective-permute-start.8
  86.3 6.7 %collective-permute-start.11 = (bf16[3,1,4,64,128]{4,3,2,1,0:T(8,128)(2,1)S(1)}, bf16[3,1,4,64,128]{4,3,2,1,0:T(8,128)(2,1)S(1)}, u32[]{:S(2)}, u32[]{:S(2)}) collective-permute-start(bf16[3,1,4,64,128]{4,3,2,1,0:T(8,128)(2,1)S(1)} %pad_maximum_fusion.2), channel_id=1, source_target_pairs={{1,0},{2,1},{3,2},{4,3},{5,4},{6,5},{7,6},{8,7},{9,8},{10,9},{11,1... | collective-permute-start | bytes 589832 | tf_op jit(solution)/shard_map/ppermute | solution.py:18
  88.2 10.5 %collective-permute-start.10 = (bf16[3,1,4,64,128]{4,3,2,1,0:T(8,128)(2,1)S(1)}, bf16[3,1,4,64,128]{4,3,2,1,0:T(8,128)(2,1)S(1)}, u32[]{:S(2)}, u32[]{:S(2)}) collective-permute-start(bf16[3,1,4,64,128]{4,3,2,1,0:T(8,128)(2,1)S(1)} %pad_maximum_fusion.2), channel_id=1, source_target_pairs={{0,1},{1,2},{2,3},{3,4},{4,5},{5,6},{6,7},{7,8},{8,9},{9,10},{10,1... | collective-permute-start | bytes 589832 | tf_op jit(solution)/shard_map/ppermute | solution.py:16
  100.7 13.9 %collective-permute-start.13 = (bf16[1,1,4,64,128]{4,3,2,1,0:T(8,128)(2,1)S(1)}, bf16[1,1,4,64,128]{4,3,2,1,0:T(8,128)(2,1)S(1)}, u32[]{:S(2)}, u32[]{:S(2)}) collective-permute-start(bf16[1,1,4,64,128]{4,3,2,1,0:T(8,128)(2,1)S(1)} %convert_bitcast_fusion.2), channel_id=1, source_target_pairs={{32,0},{64,32},{96,64},{128,96},{160,128},{192,160},{224,192},{256... | collective-permute-start | bytes 196616 | tf_op jit(solution)/shard_map/ppermute | solution.py:18
  112.7 3.2 collective-permute-start.12
  116.0 6.7 %collective-permute-start.15 = (bf16[3,1,4,64,128]{4,3,2,1,0:T(8,128)(2,1)S(1)}, bf16[3,1,4,64,128]{4,3,2,1,0:T(8,128)(2,1)S(1)}, u32[]{:S(2)}, u32[]{:S(2)}) collective-permute-start(bf16[3,1,4,64,128]{4,3,2,1,0:T(8,128)(2,1)S(1)} %pad_maximum_fusion.3), channel_id=1, source_target_pairs={{1,0},{2,1},{3,2},{4,3},{5,4},{6,5},{7,6},{8,7},{9,8},{10,9},{11,1... | collective-permute-start | bytes 589832 | tf_op jit(solution)/shard_map/ppermute | solution.py:18
  117.9 10.5 %collective-permute-start.14 = (bf16[3,1,4,64,128]{4,3,2,1,0:T(8,128)(2,1)S(1)}, bf16[3,1,4,64,128]{4,3,2,1,0:T(8,128)(2,1)S(1)}, u32[]{:S(2)}, u32[]{:S(2)}) collective-permute-start(bf16[3,1,4,64,128]{4,3,2,1,0:T(8,128)(2,1)S(1)} %pad_maximum_fusion.3), channel_id=1, source_target_pairs={{0,1},{1,2},{2,3},{3,4},{4,5},{5,6},{6,7},{7,8},{8,9},{9,10},{10,1... | collective-permute-start | bytes 589832 | tf_op jit(solution)/shard_map/ppermute | solution.py:16
  130.4 14.9 %collective-permute-start.17 = (bf16[1,1,4,64,128]{4,3,2,1,0:T(8,128)(2,1)S(1)}, bf16[1,1,4,64,128]{4,3,2,1,0:T(8,128)(2,1)S(1)}, u32[]{:S(2)}, u32[]{:S(2)}) collective-permute-start(bf16[1,1,4,64,128]{4,3,2,1,0:T(8,128)(2,1)S(1)} %get-tuple-element.22), channel_id=1, source_target_pairs={{32,0},{64,32},{96,64},{128,96},{160,128},{192,160},{224,192},{256... | collective-permute-start | bytes 196616 | tf_op jit(solution)/shard_map/ppermute | solution.py:18
  143.4 3.2 collective-permute-start.16
  146.7 6.7 %collective-permute-start.19 = (bf16[3,1,4,64,128]{4,3,2,1,0:T(8,128)(2,1)S(1)}, bf16[3,1,4,64,128]{4,3,2,1,0:T(8,128)(2,1)S(1)}, u32[]{:S(2)}, u32[]{:S(2)}) collective-permute-start(bf16[3,1,4,64,128]{4,3,2,1,0:T(8,128)(2,1)S(1)} %pad_maximum_fusion.4), channel_id=1, source_target_pairs={{1,0},{2,1},{3,2},{4,3},{5,4},{6,5},{7,6},{8,7},{9,8},{10,9},{11,1... | collective-permute-start | bytes 589832 | tf_op jit(solution)/shard_map/ppermute | solution.py:18
  148.6 10.5 %collective-permute-start.18 = (bf16[3,1,4,64,128]{4,3,2,1,0:T(8,128)(2,1)S(1)}, bf16[3,1,4,64,128]{4,3,2,1,0:T(8,128)(2,1)S(1)}, u32[]{:S(2)}, u32[]{:S(2)}) collective-permute-start(bf16[3,1,4,64,128]{4,3,2,1,0:T(8,128)(2,1)S(1)} %pad_maximum_fusion.4), channel_id=1, source_target_pairs={{0,1},{1,2},{2,3},{3,4},{4,5},{5,6},{6,7},{7,8},{8,9},{9,10},{10,1... | collective-permute-start | bytes 589832 | tf_op jit(solution)/shard_map/ppermute | solution.py:16
  161.1 14.9 %collective-permute-start.21 = (bf16[1,1,4,64,128]{4,3,2,1,0:T(8,128)(2,1)S(1)}, bf16[1,1,4,64,128]{4,3,2,1,0:T(8,128)(2,1)S(1)}, u32[]{:S(2)}, u32[]{:S(2)}) collective-permute-start(bf16[1,1,4,64,128]{4,3,2,1,0:T(8,128)(2,1)S(1)} %convert_bitcast_fusion.1), channel_id=1, source_target_pairs={{32,0},{64,32},{96,64},{128,96},{160,128},{192,160},{224,192},{256... | collective-permute-start | bytes 196616 | tf_op jit(solution)/shard_map/ppermute | solution.py:18
  174.1 3.2 collective-permute-start.20
  177.4 6.7 %collective-permute-start.23 = (bf16[3,1,4,64,128]{4,3,2,1,0:T(8,128)(2,1)S(1)}, bf16[3,1,4,64,128]{4,3,2,1,0:T(8,128)(2,1)S(1)}, u32[]{:S(2)}, u32[]{:S(2)}) collective-permute-start(bf16[3,1,4,64,128]{4,3,2,1,0:T(8,128)(2,1)S(1)} %pad_maximum_fusion.5), channel_id=1, source_target_pairs={{1,0},{2,1},{3,2},{4,3},{5,4},{6,5},{7,6},{8,7},{9,8},{10,9},{11,1... | collective-permute-start | bytes 589832 | tf_op jit(solution)/shard_map/ppermute | solution.py:18
  179.3 10.5 %collective-permute-start.22 = (bf16[3,1,4,64,128]{4,3,2,1,0:T(8,128)(2,1)S(1)}, bf16[3,1,4,64,128]{4,3,2,1,0:T(8,128)(2,1)S(1)}, u32[]{:S(2)}, u32[]{:S(2)}) collective-permute-start(bf16[3,1,4,64,128]{4,3,2,1,0:T(8,128)(2,1)S(1)} %pad_maximum_fusion.5), channel_id=1, source_target_pairs={{0,1},{1,2},{2,3},{3,4},{4,5},{5,6},{6,7},{7,8},{8,9},{9,10},{10,1... | collective-permute-start | bytes 589832 | tf_op jit(solution)/shard_map/ppermute | solution.py:16
  191.8 14.9 %collective-permute-start.25 = (bf16[1,1,4,64,128]{4,3,2,1,0:T(8,128)(2,1)S(1)}, bf16[1,1,4,64,128]{4,3,2,1,0:T(8,128)(2,1)S(1)}, u32[]{:S(2)}, u32[]{:S(2)}) collective-permute-start(bf16[1,1,4,64,128]{4,3,2,1,0:T(8,128)(2,1)S(1)} %get-tuple-element.24), channel_id=1, source_target_pairs={{32,0},{64,32},{96,64},{128,96},{160,128},{192,160},{224,192},{256... | collective-permute-start | bytes 196616 | tf_op jit(solution)/shard_map/ppermute | solution.py:18
  204.8 3.2 collective-permute-start.24
  208.0 6.7 %collective-permute-start.27 = (bf16[3,1,4,64,128]{4,3,2,1,0:T(8,128)(2,1)S(1)}, bf16[3,1,4,64,128]{4,3,2,1,0:T(8,128)(2,1)S(1)}, u32[]{:S(2)}, u32[]{:S(2)}) collective-permute-start(bf16[3,1,4,64,128]{4,3,2,1,0:T(8,128)(2,1)S(1)} %pad_maximum_fusion.6), channel_id=1, source_target_pairs={{1,0},{2,1},{3,2},{4,3},{5,4},{6,5},{7,6},{8,7},{9,8},{10,9},{11,1... | collective-permute-start | bytes 589832 | tf_op jit(solution)/shard_map/ppermute | solution.py:18
  210.0 10.5 %collective-permute-start.26 = (bf16[3,1,4,64,128]{4,3,2,1,0:T(8,128)(2,1)S(1)}, bf16[3,1,4,64,128]{4,3,2,1,0:T(8,128)(2,1)S(1)}, u32[]{:S(2)}, u32[]{:S(2)}) collective-permute-start(bf16[3,1,4,64,128]{4,3,2,1,0:T(8,128)(2,1)S(1)} %pad_maximum_fusion.6), channel_id=1, source_target_pairs={{0,1},{1,2},{2,3},{3,4},{4,5},{5,6},{6,7},{7,8},{8,9},{9,10},{10,1... | collective-permute-start | bytes 589832 | tf_op jit(solution)/shard_map/ppermute | solution.py:16
  222.5 15.1 %collective-permute-start.29 = (bf16[1,1,4,64,128]{4,3,2,1,0:T(8,128)(2,1)S(1)}, bf16[1,1,4,64,128]{4,3,2,1,0:T(8,128)(2,1)S(1)}, u32[]{:S(2)}, u32[]{:S(2)}) collective-permute-start(bf16[1,1,4,64,128]{4,3,2,1,0:T(8,128)(2,1)S(1)} %convert_bitcast_fusion), channel_id=1, source_target_pairs={{32,0},{64,32},{96,64},{128,96},{160,128},{192,160},{224,192},{256... | collective-permute-start | bytes 196616 | tf_op jit(solution)/shard_map/ppermute | solution.py:18
  235.5 3.2 collective-permute-start.28
  238.8 6.7 %collective-permute-start.31 = (bf16[3,1,4,64,128]{4,3,2,1,0:T(8,128)(2,1)S(1)}, bf16[3,1,4,64,128]{4,3,2,1,0:T(8,128)(2,1)S(1)}, u32[]{:S(2)}, u32[]{:S(2)}) collective-permute-start(bf16[3,1,4,64,128]{4,3,2,1,0:T(8,128)(2,1)S(1)} %pad_maximum_fusion.7), channel_id=1, source_target_pairs={{1,0},{2,1},{3,2},{4,3},{5,4},{6,5},{7,6},{8,7},{9,8},{10,9},{11,1... | collective-permute-start | bytes 589832 | tf_op jit(solution)/shard_map/ppermute | solution.py:18
  240.7 10.5 %collective-permute-start.30 = (bf16[3,1,4,64,128]{4,3,2,1,0:T(8,128)(2,1)S(1)}, bf16[3,1,4,64,128]{4,3,2,1,0:T(8,128)(2,1)S(1)}, u32[]{:S(2)}, u32[]{:S(2)}) collective-permute-start(bf16[3,1,4,64,128]{4,3,2,1,0:T(8,128)(2,1)S(1)} %pad_maximum_fusion.7), channel_id=1, source_target_pairs={{0,1},{1,2},{2,3},{3,4},{4,5},{5,6},{6,7},{7,8},{8,9},{9,10},{10,1... | collective-permute-start | bytes 589832 | tf_op jit(solution)/shard_map/ppermute | solution.py:16
  (3 other events, 34.1 us)
where the time goes:
time: 362 us; the launch traced here: 361 us
  starting transfers between devices  161 us (44%)
  blocking collectives  103 us (28%)
  waiting for transfers between devices  70 us (19%)
  matrix products  14 us (4%)
  local copies, waits for them, and re-layouts  6.08 us (2%)
  other arithmetic  4.44 us (1%)
    ppermute x16, starting transfers between devices, extended_2(): lax.ppermute(head, axis, [((i + 1) % count, i) for i in range(count)])  120 us
    psum x1, blocking collectives, summed_now(): return lax.psum(partial_moment, ('gx', 'gy'))  103 us
    ppermute x16, waiting for transfers between devices, extended_2(): lax.ppermute(tail, axis, [(i, (i + 1) % count) for i in range(count)])  60.6 us
    ppermute x16, starting transfers between devices, extended_2(): lax.ppermute(tail, axis, [(i, (i + 1) % count) for i in range(count)])  41 us
    dot_general x8, matrix products, apply_operator(): jnp.einsum('xyzocs,xyzors->xyzcr', stacked, ordered, preferred_element_ty...  10.8 us
    ppermute x16, waiting for transfers between devices, extended_2(): lax.ppermute(head, axis, [((i + 1) % count, i) for i in range(count)])  9.41 us
  transfers between devices with their start and end apart: 32, of which 23 were waited for; matrix products, arithmetic and copies ran while one was open for 1% of the time, Pallas kernels for 0%

commit v1 on v0

v1 whole, which is shorter than its diff:
```python
import jax
import jax.numpy as jnp
from jax import lax
from jax.experimental import pallas as pl
from jax.experimental.pallas import tpu as pltpu
from jax.sharding import PartitionSpec as P

STEPS = 8
TILE = 128
DEPTH = 4
CODES = 27
CHUNKS = 2
HALF = 32
ROWS = HALF // CHUNKS
WIDE = DEPTH * TILE
NX, NY = 16, 32
MESH = pl.DeviceIdType.MESH

MESSAGES = (
    (1, 0, 1, 1, 2),
    (-1, 0, 0, 1, 3),
    (1, 1, 1, 1, 4),
    (1, -1, 1, 1, 5),
    (-1, 1, 0, 1, 6),
    (-1, -1, 0, 1, 7),
    (0, 1, 0, 2, 8),
    (0, -1, 0, 2, 10),
)
SLOTS = 12
SOURCES = ((4, 2, 5, 8, 0, 10, 9, 1, 11), (8, 0, 10, 9, 1, 11, 6, 3, 7))
GROUP_A, GROUP_B = 16, 32


def kernel(
    inverse, start_hbm, blocks_hbm, moments_ref, last_ref,
    start, blocks, mats, buf, vecs, first, staged, landed, sums, turned, pay, gather_a, gather_b,
    load_sem, send, recv, pair_send, pair_recv, a_send, a_recv, b_send, b_recv,
):
    gx, gy = lax.axis_index("gx"), lax.axis_index("gy")
    core = lax.rem(gx, 2)
    other = 1 - core
    chip = gx - core
    z_hi, col_x = gx // 8, lax.rem(gx, 8) // 2
    col_y, z_lo = gy // 4, lax.rem(gy, 4)
    in_a = (z_hi * 4 + z_lo) * 2 + core
    in_b = col_y * 4 + col_x

    def neighbour(dx, dy):
        return (lax.rem(gx + 2 * dx + NX, NX), lax.rem(gy + dy + NY, NY))

    def member_a(m):
        z = m // 2
        return ((z // 4) * 8 + col_x * 2 + lax.rem(m, 2), col_y * 4 + lax.rem(z, 4))

    def member_b(m):
        return (z_hi * 8 + lax.rem(m, 4) * 2 + core, (m // 4) * 4 + z_lo)

    load_vecs = pltpu.make_async_copy(start_hbm, start, load_sem.at[0])
    load_blocks = pltpu.make_async_copy(blocks_hbm, blocks, load_sem.at[1])
    load_vecs.start()
    load_blocks.start()

    barrier = pltpu.get_barrier_semaphore()
    for dx, dy, _, _, _ in MESSAGES:
        pl.semaphore_signal(barrier, inc=1, device_id=neighbour(dx, dy), device_id_type=MESH)

    def greet_a(d, c):
        pl.semaphore_signal(
            barrier, inc=1, device_id=member_a(lax.rem(in_a + d, GROUP_A)), device_id_type=MESH
        )
        return c

    def greet_b(d, c):
        pl.semaphore_signal(
            barrier, inc=1, device_id=member_b(lax.rem(in_b + d, GROUP_B)), device_id_type=MESH
        )
        return c

    lax.fori_loop(1, GROUP_A, greet_a, 0)
    lax.fori_loop(1, GROUP_B, greet_b, 0)

    turned[...] = jnp.zeros_like(turned)
    pay[...] = jnp.zeros_like(pay)
    load_vecs.wait()
    for ch in range(CHUNKS):
        for z in range(DEPTH):
            lanes = slice(z * TILE, (z + 1) * TILE)
            mine = pl.ds(pl.multiple_of(core * HALF + ch * ROWS, ROWS), ROWS)
            theirs = pl.ds(pl.multiple_of(other * HALF + ch * ROWS, ROWS), ROWS)
            first[core, ch, :, lanes] = start[z, mine, :]
            staged[ch, :, lanes] = start[z, theirs, :]

    load_blocks.wait()
    blank = jnp.zeros((TILE, TILE), jnp.bfloat16)
    for j in range(9):
        for z in range(DEPTH):
            part, row = z // 2, (z % 2) * TILE
            for window in range(3):
                dz = part + window - z
                if -1 <= dz <= 1:
                    block = blocks[z * CODES + inverse[z, j * 3 + dz + 1]]
                else:
                    block = blank
                mats[core, j, part, row : row + TILE, window * TILE : (window + 1) * TILE] = block

    pl.semaphore_wait(barrier, len(MESSAGES) + GROUP_A - 1 + GROUP_B - 1)

    partner = (chip + other, gy)
    give_vecs = pltpu.make_async_remote_copy(
        src_ref=staged, dst_ref=first.at[core], send_sem=pair_send.at[0], recv_sem=pair_recv.at[0],
        device_id=partner, device_id_type=MESH,
    )
    give_vecs.start()
    give_mats = pltpu.make_async_remote_copy(
        src_ref=mats.at[core], dst_ref=mats.at[core], send_sem=pair_send.at[1], recv_sem=pair_recv.at[1],
        device_id=partner, device_id_type=MESH,
    )

    def copies(p, ch):
        return [
            pltpu.make_async_remote_copy(
                src_ref=buf.at[p, ch, lo : lo + count],
                dst_ref=buf.at[p, ch, slot : slot + count],
                send_sem=send.at[p, ch, i],
                recv_sem=recv.at[p, ch, i],
                device_id=neighbour(dx, dy),
                device_id_type=MESH,
            )
            for i, (dx, dy, lo, count, slot) in enumerate(MESSAGES)
        ]

    def fold(value):
        return sum(value[:, z * TILE : (z + 1) * TILE] for z in range(DEPTH))

    def row_of_sums():
        return jnp.sum(jnp.transpose(turned[...]), axis=0, keepdims=True)

    give_vecs.wait_recv()
    for ch in range(CHUNKS):
        for a in range(2):
            buf[0, ch, a] = first[a, ch].astype(jnp.bfloat16)
        for copy in copies(0, ch):
            copy.start()
    give_mats.start()
    for ch in range(CHUNKS):
        total = jnp.zeros((ROWS, TILE), jnp.float32)
        for a in range(2):
            value = first[a, ch]
            vecs[0, a, ch] = value
            vecs[1, a, ch] = jnp.zeros_like(value)
            total = total + fold(value * value)
        turned[ch * ROWS : (ch + 1) * ROWS, :] = total
    rows_8 = lax.broadcasted_iota(jnp.int32, (8, TILE), 0)
    pay[...] = jnp.where(rows_8 == 0, row_of_sums(), 0.0)
    give_mats.wait_recv()

    def step(n, carry):
        p = lax.rem(n, 2)
        q = 1 - p
        scale = jnp.where(n == 0, 1.0, 2.0).astype(jnp.float32)
        for ch in range(CHUNKS):
            for copy in copies(p, ch):
                copy.wait_recv()

            @pl.when(n >= 1)
            def _():
                for copy in copies(q, ch):
                    copy.wait_send()

            total = jnp.zeros((ROWS, TILE), jnp.float32)
            for a in range(2):
                for part in range(2):
                    acc = jnp.zeros((ROWS, 2 * TILE), jnp.float32)
                    for j in range(9):
                        acc = acc + lax.dot_general(
                            buf[p, ch, SOURCES[a][j], :, part * TILE : (part + 3) * TILE],
                            mats[a, j, part],
                            (((1,), (1,)), ((), ())),
                            preferred_element_type=jnp.float32,
                        )
                    lanes = slice(part * 2 * TILE, (part + 1) * 2 * TILE)
                    value = scale * acc - vecs[q, a, ch, :, lanes]
                    vecs[q, a, ch, :, lanes] = value
                    buf[q, ch, a, :, lanes] = value.astype(jnp.bfloat16)
                    product = value * first[a, ch, :, lanes]
                    total = total + product[:, :TILE] + product[:, TILE:]

            @pl.when(n < STEPS - 1)
            def _():
                for copy in copies(q, ch):
                    copy.start()

            turned[ch * ROWS : (ch + 1) * ROWS, :] = total

        @pl.when(n < STEPS - 1)
        def _():
            pay[...] = jnp.where(rows_8 == n + 1, row_of_sums(), pay[...])

        return carry

    lax.fori_loop(0, STEPS, step, 0)

    final = STEPS % 2
    give_last = pltpu.make_async_remote_copy(
        src_ref=vecs.at[final, other], dst_ref=landed, send_sem=pair_send.at[2], recv_sem=pair_recv.at[2],
        device_id=partner, device_id_type=MESH,
    )
    give_last.start()

    eighth = pltpu.roll(jnp.broadcast_to(row_of_sums(), (8, TILE)), HALF, 1)
    lanes_8 = lax.broadcasted_iota(jnp.int32, (8, TILE), 1)
    put = (rows_8 == 0) & (lanes_8 >= HALF) & (lanes_8 < 2 * HALF)
    sums[0] = jnp.where(put, eighth, pay[...])

    def share(source, gathered, me, member, size, sent, received):
        def to(d):
            return pltpu.make_async_remote_copy(
                src_ref=source, dst_ref=gathered.at[me], send_sem=sent.at[d], recv_sem=received.at[me],
                device_id=member(lax.rem(me + d, size)), device_id_type=MESH,
            )

        def begin(d, c):
            to(d).start()
            return c

        def finish(d, c):
            who = lax.rem(me + d, size)
            pltpu.make_async_remote_copy(
                src_ref=source, dst_ref=gathered.at[who], send_sem=sent.at[d], recv_sem=received.at[who],
                device_id=member(who), device_id_type=MESH,
            ).wait_recv()
            return c

        def done(d, c):
            to(d).wait_send()
            return c

        lax.fori_loop(1, size, begin, 0)
        gathered[me] = source[...]
        lax.fori_loop(1, size, finish, 0)
        result = jnp.sum(gathered[...], axis=0)
        return result, lambda: lax.fori_loop(1, size, done, 0)

    result_a, done_a = share(sums.at[0], gather_a, in_a, member_a, GROUP_A, a_send, a_recv)
    sums[1] = result_a
    result_b, done_b = share(sums.at[1], gather_b, in_b, member_b, GROUP_B, b_send, b_recv)
    scaled = result_b * (1.0 / (NX * NY * DEPTH * TILE))
    moments_ref[0:8, :] = scaled[:, :HALF]
    moments_ref[8:9, :] = pltpu.roll(scaled, TILE - HALF, 1)[0:1, :HALF]

    give_last.wait_recv()
    for ch in range(CHUNKS):
        for z in range(DEPTH):
            lanes = slice(z * TILE, (z + 1) * TILE)
            mine = pl.ds(pl.multiple_of(core * HALF + ch * ROWS, ROWS), ROWS)
            theirs = pl.ds(pl.multiple_of(other * HALF + ch * ROWS, ROWS), ROWS)
            last_ref[z, mine, :] = vecs[final, core, ch, :, lanes]
            last_ref[z, theirs, :] = landed[ch, :, lanes]

    done_a()
    done_b()
    for copy in (give_vecs, give_mats, give_last):
        copy.wait_send()
    for ch in range(CHUNKS):
        for copy in copies((STEPS - 1) % 2, ch):
            copy.wait_send()


def body(start_vecs, force_blocks, slot_offsets):
    codes = lax.broadcasted_iota(jnp.int32, (DEPTH, CODES, CODES), 2)
    slots = lax.broadcasted_iota(jnp.int32, (DEPTH, CODES, CODES), 1)
    match = slot_offsets.reshape(DEPTH, CODES)[:, :, None] == codes
    inverse = jnp.sum(jnp.where(match, slots, 0), axis=1).astype(jnp.int32)
    vec_shape = (2, CHUNKS, ROWS, WIDE)
    count = len(MESSAGES)
    moments, last = pl.pallas_call(
        kernel,
        out_shape=(
            jax.ShapeDtypeStruct((STEPS + 1, HALF), jnp.float32),
            jax.ShapeDtypeStruct((DEPTH, 2 * HALF, TILE), jnp.float32),
        ),
        in_specs=[
            pl.BlockSpec(memory_space=pltpu.SMEM),
            pl.BlockSpec(memory_space=pl.ANY),
            pl.BlockSpec(memory_space=pl.ANY),
        ],
        out_specs=(pl.BlockSpec(memory_space=pltpu.VMEM), pl.BlockSpec(memory_space=pltpu.VMEM)),
        scratch_shapes=[
            pltpu.VMEM((DEPTH, 2 * HALF, TILE), jnp.float32),
            pltpu.VMEM((DEPTH * CODES, TILE, TILE), jnp.bfloat16),
            pltpu.VMEM((2, 9, 2, 2 * TILE, 3 * TILE), jnp.bfloat16),
            pltpu.VMEM((2, CHUNKS, SLOTS, ROWS, WIDE), jnp.bfloat16),
            pltpu.VMEM((2,) + vec_shape, jnp.float32),
            pltpu.VMEM(vec_shape, jnp.float32),
            pltpu.VMEM(vec_shape[1:], jnp.float32),
            pltpu.VMEM(vec_shape[1:], jnp.float32),
            pltpu.VMEM((2, 8, TILE), jnp.float32),
            pltpu.VMEM((TILE, TILE), jnp.float32),
            pltpu.VMEM((8, TILE), jnp.float32),
            pltpu.VMEM((GROUP_A, 8, TILE), jnp.float32),
            pltpu.VMEM((GROUP_B, 8, TILE), jnp.float32),
            pltpu.SemaphoreType.DMA((2,)),
            pltpu.SemaphoreType.DMA((2, CHUNKS, count)),
            pltpu.SemaphoreType.DMA((2, CHUNKS, count)),
            pltpu.SemaphoreType.DMA((3,)),
            pltpu.SemaphoreType.DMA((3,)),
            pltpu.SemaphoreType.DMA((GROUP_A,)),
            pltpu.SemaphoreType.DMA((GROUP_A,)),
            pltpu.SemaphoreType.DMA((GROUP_B,)),
            pltpu.SemaphoreType.DMA((GROUP_B,)),
        ],
        compiler_params=pltpu.CompilerParams(
            collective_id=0, has_side_effects=True, vmem_limit_bytes=32 << 20
        ),
    )(
        inverse,
        start_vecs.reshape(DEPTH, 2 * HALF, TILE),
        force_blocks.reshape(DEPTH * CODES, TILE, TILE),
    )
    return moments, last.reshape(1, 1, DEPTH, 2 * HALF, TILE)


def solution(mesh):
    in_specs = (
        P("gx", "gy", None, None, None),
        P("gx", "gy", None, None, None, None),
        P("gx", "gy", None, None),
    )
    out_specs = (P(), P("gx", "gy", None, None, None))
    return jax.shard_map(body, mesh=mesh, in_specs=in_specs, out_specs=out_specs, check_vma=False)
```

time: 362 us -> 123 us (0.34)
  starting transfers between devices: 161 us -> 0 us
  Pallas kernels: 0 us -> 117 us
  blocking collectives: 103 us -> 0 us
  waiting for transfers between devices: 70 us -> 0 us
  matrix products: 14 us -> 0 us
  other arithmetic: 4.44 us -> 0.1 us
    ppermute x32 -> x0, starting transfers between devices: 161 us -> none  [the longest x16 120 us: extended_2(): lax.ppermute(head, axis, [((i + 1) % count, i) for i in range(count)])]
    pallas_call x0 -> x1, Pallas kernels: none -> 117 us  [body(): pl.pallas_call(kernel, out_shape=(jax.ShapeDtypeStruct((STEPS + 1, HALF),...]
    psum x1 -> x0, blocking collectives: 103 us -> none  [summed_now(): return lax.psum(partial_moment, ('gx', 'gy'))]
    ppermute x32 -> x0, waiting for transfers between devices: 70 us -> none  [the longest x16 60.6 us: extended_2(): lax.ppermute(tail, axis, [(i, (i + 1) % count) for i in range(count)])]
    dot_general x9 -> x0, matrix products: 14 us -> none  [the longest x8 10.8 us: apply_operator(): jnp.einsum('xyzocs,xyzors->xyzcr', stacked, ordered, preferred_element_ty...]
  transfers between devices with their start and end apart: 32 -> 0, of which waited for: 23 -> 0; matrix products, arithmetic and copies ran while one was open for 1% -> 0% of each run, Pallas kernels for 0% -> 0%
where the time goes in v1:
time: 123 us; the launch traced here: 122 us
  Pallas kernels  117 us (95%)
  local copies, waits for them, and re-layouts  4.93 us (4%)
    pallas_call x1, Pallas kernels, body(): pl.pallas_call(kernel, out_shape=(jax.ShapeDtypeStruct((STEPS + 1, HALF),...  117 us
    unnamed x6, local copies, waits for them, and re-layouts  4.16 us

profile of v1, /device:TPU:1, one launch (start us, length us, event | category | flops | bytes accessed | tf_op | source)
XLA Modules:
  0.0 122.3 jit_solution(18023553067148665765)
XLA Ops:
  0.6 0.8 copy.5
  1.4 0.1 select_reduce_fusion.inverse
  1.5 0.0 copy-start
  1.5 2.0 %copy-done = bf16[1,1,4,27,128,128]{5,4,3,2,1,0:T(8,128)(2,1)S(1)} copy-done((bf16[1,1,4,27,128,128]{5,4,3,2,1,0:T(8,128)(2,1)S(1)}, bf16[1,1,4,27,128,128]{5,4,3,2,1,0:T(8,128)(2,1)}, u32[]{:S(2)}) %copy-start) | copy-done | bytes 3538968
  3.5 0.0 copy-start.1
  3.5 0.9 copy-done.1
  4.4 116.7 %shard_map.50 = (f32[9,32]{1,0:T(8,128)S(1)}, f32[4,64,128]{2,1,0:T(8,128)S(1)}) custom-call(s32[4,27]{1,0:T(4,128)S(1)} %select_reduce_fusion.inverse, f32[4,64,128]{2,1,0:T(8,128)S(1)} %bitcast.5, bf16[108,128,128]{2,1,0:T(8,128)(2,1)S(1)} %bitcast.4), custom_call_target="tpu_custom_call" | custom-call | tf_op jit(solution)/shard_map/pallas_call | solution.py:276
  121.1 0.6 copy.8
  121.7 0.7 copy.9
Async XLA Ops:
  1.5 2.0 %copy-start = (bf16[1,1,4,27,128,128]{5,4,3,2,1,0:T(8,128)(2,1)S(1)}, bf16[1,1,4,27,128,128]{5,4,3,2,1,0:T(8,128)(2,1)}, u32[]{:S(2)}) copy-start(bf16[1,1,4,27,128,128]{5,4,3,2,1,0:T(8,128)(2,1)} %param.4) | copy-start | bytes 10616836
  3.5 0.9 copy-start.1

commit v2 on v1

--- a/solution.py
+++ b/solution.py
@@ -27,12 +27,18 @@
     (0, -1, 0, 2, 10),
 )
 SLOTS = 12
-SOURCES = ((4, 2, 5, 8, 0, 10, 9, 1, 11), (8, 0, 10, 9, 1, 11, 6, 3, 7))
+SOURCES = ((0, 1, 8, 9, 10, 11, 2, 4, 5), (0, 1, 8, 9, 10, 11, 3, 6, 7))
+PLACES = ((4, 7, 3, 6, 5, 8, 1, 0, 2), (1, 4, 0, 3, 2, 5, 7, 6, 8))
+GROUPS = (((), 0, 2), ((6, 7), 2, 6), ((0, 1, 2, 3, 4, 5), 6, 9))
 GROUP_A, GROUP_B = 16, 32
 
 
+def window(z):
+    return max(z - 1, 0), min(z + 2, DEPTH)
+
+
 def kernel(
-    inverse, start_hbm, blocks_hbm, moments_ref, last_ref,
+    offsets, start_hbm, blocks_hbm, moments_ref, last_ref,
     start, blocks, mats, buf, vecs, first, staged, landed, sums, turned, pay, gather_a, gather_b,
     load_sem, send, recv, pair_send, pair_recv, a_send, a_recv, b_send, b_recv,
 ):
@@ -90,18 +96,25 @@
             first[core, ch, :, lanes] = start[z, mine, :]
             staged[ch, :, lanes] = start[z, theirs, :]
 
+    slots = lax.broadcasted_iota(jnp.int32, (DEPTH, CODES), 1)
+    row_z = lax.broadcasted_iota(jnp.int32, (DEPTH, CODES), 0)
+    codes = offsets[...]
+    eye = jnp.where(
+        lax.broadcasted_iota(jnp.int32, (TILE, TILE), 0) == lax.broadcasted_iota(jnp.int32, (TILE, TILE), 1), 1.0, 0.0
+    ).astype(jnp.bfloat16)
     load_blocks.wait()
-    blank = jnp.zeros((TILE, TILE), jnp.bfloat16)
-    for j in range(9):
-        for z in range(DEPTH):
-            part, row = z // 2, (z % 2) * TILE
-            for window in range(3):
-                dz = part + window - z
-                if -1 <= dz <= 1:
-                    block = blocks[z * CODES + inverse[z, j * 3 + dz + 1]]
-                else:
-                    block = blank
-                mats[core, j, part, row : row + TILE, window * TILE : (window + 1) * TILE] = block
+    for z in range(DEPTH):
+        low, high = window(z)
+        for i in range(9):
+            place = jnp.where(core == 0, PLACES[0][i], PLACES[1][i])
+            for w in range(high - low):
+                code = place * 3 + low + w - z + 1
+                pick = jnp.max(jnp.where((codes == code) & (row_z == z), slots, 0))
+                block = lax.dot_general(
+                    eye, blocks[z * CODES + pick], (((1,), (1,)), ((), ())), preferred_element_type=jnp.float32
+                )
+                at = (i * (high - low) + w) * TILE
+                mats[core, z, at : at + TILE, :] = block.astype(jnp.bfloat16)
 
     pl.semaphore_wait(barrier, len(MESSAGES) + GROUP_A - 1 + GROUP_B - 1)
 
@@ -159,8 +172,20 @@
         q = 1 - p
         scale = jnp.where(n == 0, 1.0, 2.0).astype(jnp.float32)
         for ch in range(CHUNKS):
-            for copy in copies(p, ch):
-                copy.wait_recv()
+            accs = [[jnp.zeros((ROWS, TILE), jnp.float32) for _ in range(DEPTH)] for _ in range(2)]
+            arriving = copies(p, ch)
+            for waits, begin, end in GROUPS:
+                for i in waits:
+                    arriving[i].wait_recv()
+                for a in range(2):
+                    pieces = [buf[p, ch, SOURCES[a][i]] for i in range(begin, end)]
+                    for z in range(DEPTH):
+                        low, high = window(z)
+                        wide = (high - low) * TILE
+                        left = jnp.concatenate([piece[:, low * TILE : high * TILE] for piece in pieces], axis=1)
+                        accs[a][z] = accs[a][z] + jnp.dot(
+                            left, mats[a, z, begin * wide : end * wide, :], preferred_element_type=jnp.float32
+                        )
 
             @pl.when(n >= 1)
             def _():
@@ -169,21 +194,12 @@
 
             total = jnp.zeros((ROWS, TILE), jnp.float32)
             for a in range(2):
-                for part in range(2):
-                    acc = jnp.zeros((ROWS, 2 * TILE), jnp.float32)
-                    for j in range(9):
-                        acc = acc + lax.dot_general(
-                            buf[p, ch, SOURCES[a][j], :, part * TILE : (part + 3) * TILE],
-                            mats[a, j, part],
-                            (((1,), (1,)), ((), ())),
-                            preferred_element_type=jnp.float32,
-                        )
-                    lanes = slice(part * 2 * TILE, (part + 1) * 2 * TILE)
-                    value = scale * acc - vecs[q, a, ch, :, lanes]
+                for z in range(DEPTH):
+                    lanes = slice(z * TILE, (z + 1) * TILE)
+                    value = scale * accs[a][z] - vecs[q, a, ch, :, lanes]
                     vecs[q, a, ch, :, lanes] = value
                     buf[q, ch, a, :, lanes] = value.astype(jnp.bfloat16)
-                    product = value * first[a, ch, :, lanes]
-                    total = total + product[:, :TILE] + product[:, TILE:]
+                    total = total + value * first[a, ch, :, lanes]
 
             @pl.when(n < STEPS - 1)
             def _():
@@ -267,10 +283,6 @@
 
 
 def body(start_vecs, force_blocks, slot_offsets):
-    codes = lax.broadcasted_iota(jnp.int32, (DEPTH, CODES, CODES), 2)
-    slots = lax.broadcasted_iota(jnp.int32, (DEPTH, CODES, CODES), 1)
-    match = slot_offsets.reshape(DEPTH, CODES)[:, :, None] == codes
-    inverse = jnp.sum(jnp.where(match, slots, 0), axis=1).astype(jnp.int32)
     vec_shape = (2, CHUNKS, ROWS, WIDE)
     count = len(MESSAGES)
     moments, last = pl.pallas_call(
@@ -280,7 +292,7 @@
             jax.ShapeDtypeStruct((DEPTH, 2 * HALF, TILE), jnp.float32),
         ),
         in_specs=[
-            pl.BlockSpec(memory_space=pltpu.SMEM),
+            pl.BlockSpec(memory_space=pltpu.VMEM),
             pl.BlockSpec(memory_space=pl.ANY),
             pl.BlockSpec(memory_space=pl.ANY),
         ],
@@ -288,7 +300,7 @@
         scratch_shapes=[
             pltpu.VMEM((DEPTH, 2 * HALF, TILE), jnp.float32),
             pltpu.VMEM((DEPTH * CODES, TILE, TILE), jnp.bfloat16),
-            pltpu.VMEM((2, 9, 2, 2 * TILE, 3 * TILE), jnp.bfloat16),
+            pltpu.VMEM((2, DEPTH, 27 * TILE, TILE), jnp.bfloat16),
             pltpu.VMEM((2, CHUNKS, SLOTS, ROWS, WIDE), jnp.bfloat16),
             pltpu.VMEM((2,) + vec_shape, jnp.float32),
             pltpu.VMEM(vec_shape, jnp.float32),
@@ -310,10 +322,10 @@
             pltpu.SemaphoreType.DMA((GROUP_B,)),
         ],
         compiler_params=pltpu.CompilerParams(
-            collective_id=0, has_side_effects=True, vmem_limit_bytes=32 << 20
+            collective_id=0, has_side_effects=True, vmem_limit_bytes=58 << 20
         ),
     )(
-        inverse,
+        slot_offsets.reshape(DEPTH, CODES),
         start_vecs.reshape(DEPTH, 2 * HALF, TILE),
         force_blocks.reshape(DEPTH * CODES, TILE, TILE),
     )

time: 123 us -> 103 us (0.84)
  Pallas kernels: 117 us -> 99.5 us
  local copies, waits for them, and re-layouts: 4.93 us -> 2.86 us
    pallas_call x1, Pallas kernels: 117 us -> 99.5 us  [body(): pl.pallas_call(kernel, out_shape=(jax.ShapeDtypeStruct((STEPS + 1, HALF),...]
    unnamed x6 -> x2, local copies, waits for them, and re-layouts: 4.16 us -> 2.86 us
where the time goes in v2:
time: 103 us
  Pallas kernels  99.5 us (97%)
  local copies, waits for them, and re-layouts  2.86 us (3%)
    pallas_call x1, Pallas kernels, body(): pl.pallas_call(kernel, out_shape=(jax.ShapeDtypeStruct((STEPS + 1, HALF),...  99.5 us
    unnamed x2, local copies, waits for them, and re-layouts  2.86 us

profile of v2, /device:TPU:1, one launch (start us, length us, event | category | flops | bytes accessed | tf_op | source)
XLA Modules:
  0.0 103.0 jit_solution(12052208324979396572)
XLA Ops:
  0.6 99.5 %shard_map.50 = (f32[9,32]{1,0:T(8,128)}, f32[4,64,128]{2,1,0:T(8,128)}) custom-call(s32[4,27]{1,0:T(4,128)} %bitcast.7, f32[4,64,128]{2,1,0:T(8,128)} %bitcast.5, bf16[108,128,128]{2,1,0:T(8,128)(2,1)} %bitcast.4), custom_call_target="tpu_custom_call" | custom-call | tf_op jit(solution)/shard_map/pallas_call | solution.py:288
  100.1 1.3 %copy.7 = f32[9,32]{1,0:T(8,128)} copy(f32[9,32]{1,0:T(8,128)} %get-tuple-element.8) | data formatting | bytes 2304
  101.4 1.6 %copy.8 = f32[1,1,4,64,128]{4,3,2,1,0:T(8,128)} copy(f32[1,1,4,64,128]{4,3,2,1,0:T(8,128)} %bitcast.6) | data formatting | bytes 262144

commit v3 on v2

v3 whole, which is shorter than its diff:
```python
import jax
import jax.numpy as jnp
from jax import lax
from jax.experimental import pallas as pl
from jax.experimental.pallas import tpu as pltpu
from jax.sharding import PartitionSpec as P

STEPS = 8
TILE = 128
DEPTH = 4
CODES = 27
CHUNKS = 2
HALF = 32
ROWS = HALF // CHUNKS
WIDE = DEPTH * TILE
NX, NY = 16, 32
MESH = pl.DeviceIdType.MESH

MESSAGES = (
    (1, 0, 1, 1, 2),
    (-1, 0, 0, 1, 3),
    (1, 1, 1, 1, 4),
    (1, -1, 1, 1, 5),
    (-1, 1, 0, 1, 6),
    (-1, -1, 0, 1, 7),
    (0, 1, 0, 2, 8),
    (0, -1, 0, 2, 10),
)
SLOTS = 12
SOURCES = ((0, 1, 8, 9, 10, 11, 2, 4, 5), (0, 1, 8, 9, 10, 11, 3, 6, 7))
PLACES = ((4, 7, 3, 6, 5, 8, 1, 0, 2), (1, 4, 0, 3, 2, 5, 7, 6, 8))
GROUPS = (((), 0, 2), ((6, 7), 2, 6), ((0, 1, 2, 3, 4, 5), 6, 9))
GROUP_A, GROUP_B = 16, 32


def hops(step, size):
    return min(step, size - step)


STEPS_A = sorted(
    ((z, c) for z in range(8) for c in range(2) if z or c), key=lambda s: -2 * hops(s[0], 8) - s[1]
)
STEPS_B = sorted(
    ((y, x) for y in range(8) for x in range(4) if y or x), key=lambda s: -hops(s[0], 8) - hops(s[1], 4)
)


def window(z):
    return max(z - 1, 0), min(z + 2, DEPTH)


def kernel(
    offsets, start_hbm, blocks_hbm, moments_ref, last_ref,
    start, blocks, mats, buf, vecs, first, own, staged, landed, sums, turned, gather_a, gather_b,
    load_sem, send, recv, pair_send, pair_recv, a_send, a_recv, b_send, b_recv,
):
    gx, gy = lax.axis_index("gx"), lax.axis_index("gy")
    core = lax.rem(gx, 2)
    other = 1 - core
    chip = gx // 2
    half = lax.rem(core + chip + gy, 2)
    z_hi, col_x = gx // 8, lax.rem(gx, 8) // 2
    col_y, z_lo = gy // 4, lax.rem(gy, 4)
    in_a = (z_hi * 4 + z_lo) * 2 + core
    in_b = col_y * 4 + col_x

    def chip_at(dx, dy):
        return lax.rem(chip + dx + NX // 2, NX // 2), lax.rem(gy + dy + NY, NY)

    def neighbour(dx, dy):
        x, y = chip_at(dx, dy)
        return (2 * x + (core if (dx + dy) % 2 == 0 else other), y)

    def member_a(step):
        z, c = lax.rem(z_hi * 4 + z_lo + step[0], 8), lax.rem(core + step[1], 2)
        return z * 2 + c, ((z // 4) * 8 + col_x * 2 + c, col_y * 4 + lax.rem(z, 4))

    def member_b(step):
        y, x = lax.rem(col_y + step[0], 8), lax.rem(col_x + step[1], 4)
        return y * 4 + x, (z_hi * 8 + x * 2 + core, y * 4 + z_lo)

    load_vecs = pltpu.make_async_copy(start_hbm, start, load_sem.at[0])
    load_blocks = pltpu.make_async_copy(blocks_hbm, blocks, load_sem.at[1])
    load_vecs.start()
    load_blocks.start()

    barrier = pltpu.get_barrier_semaphore()

    def greet(device):
        pl.semaphore_signal(barrier, inc=1, device_id=device, device_id_type=MESH)

    for dx, dy, _, _, _ in MESSAGES:
        x, y = chip_at(dx, dy)
        for c in range(2):
            greet((2 * x + c, y))
    for step in STEPS_B:
        greet(member_b(step)[1])
    for step in STEPS_A:
        greet(member_a(step)[1])

    turned[...] = jnp.zeros_like(turned)
    load_vecs.wait()
    for ch in range(CHUNKS):
        for z in range(DEPTH):
            lanes = slice(z * TILE, (z + 1) * TILE)
            mine = pl.ds(pl.multiple_of(half * HALF + ch * ROWS, ROWS), ROWS)
            theirs = pl.ds(pl.multiple_of((1 - half) * HALF + ch * ROWS, ROWS), ROWS)
            first[core, ch, :, lanes] = start[z, mine, :]
            staged[ch, :, lanes] = start[z, theirs, :]
            for h in range(2):
                low = h * HALF + ch * ROWS
                own[h, ch, 0, :, lanes] = start[z, low : low + ROWS, :].astype(jnp.bfloat16)

    slots = lax.broadcasted_iota(jnp.int32, (DEPTH, CODES), 1)
    row_z = lax.broadcasted_iota(jnp.int32, (DEPTH, CODES), 0)
    codes = offsets[...]
    eye = jnp.where(
        lax.broadcasted_iota(jnp.int32, (TILE, TILE), 0) == lax.broadcasted_iota(jnp.int32, (TILE, TILE), 1), 1.0, 0.0
    ).astype(jnp.bfloat16)
    load_blocks.wait()
    for z in range(DEPTH):
        low, high = window(z)
        for i in range(9):
            place = jnp.where(core == 0, PLACES[0][i], PLACES[1][i])
            for w in range(high - low):
                code = place * 3 + low + w - z + 1
                pick = jnp.max(jnp.where((codes == code) & (row_z == z), slots, 0))
                block = lax.dot_general(
                    eye, blocks[z * CODES + pick], (((1,), (1,)), ((), ())), preferred_element_type=jnp.float32
                )
                at = (i * (high - low) + w) * TILE
                mats[core, z, at : at + TILE, :] = block.astype(jnp.bfloat16)

    pl.semaphore_wait(barrier, 2 * len(MESSAGES) + GROUP_A - 1 + GROUP_B - 1)

    side = 2 * core - 1
    first_sends = []
    for dx, dy, slot, receives, sends in (
        (side, 0, 3 - core, 1 - core, (0, 1)),
        (side, 1, 6 - 2 * core, 4 - 2 * core, (2, 3)),
        (side, -1, 7 - 2 * core, 5 - 2 * core, (4, 5)),
        (0, 1, 8 + core, 6, (6, 6)),
        (0, -1, 10 + core, 7, (7, 7)),
    ):
        x, y = chip_at(dx, dy)
        for c in range(2):
            first_sends.append((2 * x + c, y, lax.rem(c + x + y, 2), slot, receives, sends[c]))
    for ch in range(CHUNKS):
        for x, y, h, slot, receives, sends in first_sends:
            pltpu.make_async_remote_copy(
                src_ref=own.at[h, ch],
                dst_ref=buf.at[0, ch, pl.ds(slot, 1)],
                send_sem=send.at[0, ch, sends],
                recv_sem=recv.at[0, ch, receives],
                device_id=(x, y),
                device_id_type=MESH,
            ).start()

    partner = (2 * chip + other, gy)
    give_vecs = pltpu.make_async_remote_copy(
        src_ref=staged, dst_ref=first.at[core], send_sem=pair_send.at[0], recv_sem=pair_recv.at[0],
        device_id=partner, device_id_type=MESH,
    )
    give_vecs.start()
    give_mats = pltpu.make_async_remote_copy(
        src_ref=mats.at[core], dst_ref=mats.at[core], send_sem=pair_send.at[1], recv_sem=pair_recv.at[1],
        device_id=partner, device_id_type=MESH,
    )

    def copies(p, ch):
        return [
            pltpu.make_async_remote_copy(
                src_ref=buf.at[p, ch, lo : lo + count],
                dst_ref=buf.at[p, ch, slot : slot + count],
                send_sem=send.at[p, ch, i],
                recv_sem=recv.at[p, ch, i],
                device_id=neighbour(dx, dy),
                device_id_type=MESH,
            )
            for i, (dx, dy, lo, count, slot) in enumerate(MESSAGES)
        ]

    def fold(value):
        return sum(value[:, z * TILE : (z + 1) * TILE] for z in range(DEPTH))

    def row_of_sums(i):
        return jnp.sum(jnp.transpose(turned[i]), axis=0, keepdims=True)

    give_mats.start()
    give_vecs.wait_recv()
    for ch in range(CHUNKS):
        total = jnp.zeros((ROWS, TILE), jnp.float32)
        for a in range(2):
            value = first[a, ch]
            buf[0, ch, a] = value.astype(jnp.bfloat16)
            vecs[0, a, ch] = value
            vecs[1, a, ch] = jnp.zeros_like(value)
            total = total + fold(value * value)
        turned[0, ch * ROWS : (ch + 1) * ROWS, :] = total
    give_mats.wait_recv()

    def step(n, carry):
        p = lax.rem(n, 2)
        q = 1 - p
        scale = jnp.where(n == 0, 1.0, 2.0).astype(jnp.float32)

        for ch in range(CHUNKS):
            accs = [[jnp.zeros((ROWS, TILE), jnp.float32) for _ in range(DEPTH)] for _ in range(2)]
            arriving = copies(p, ch)
            for waits, begin, end in GROUPS:
                for i in waits:
                    arriving[i].wait_recv()
                for a in range(2):
                    pieces = [buf[p, ch, SOURCES[a][i]] for i in range(begin, end)]
                    for z in range(DEPTH):
                        low, high = window(z)
                        wide = (high - low) * TILE
                        left = jnp.concatenate([piece[:, low * TILE : high * TILE] for piece in pieces], axis=1)
                        accs[a][z] = accs[a][z] + jnp.dot(
                            left, mats[a, z, begin * wide : end * wide, :], preferred_element_type=jnp.float32
                        )

            @pl.when(n >= 1)
            def _():
                for copy in copies(q, ch):
                    copy.wait_send()

            for a in range(2):
                for z in range(DEPTH):
                    lanes = slice(z * TILE, (z + 1) * TILE)
                    value = scale * accs[a][z] - vecs[q, a, ch, :, lanes]
                    vecs[q, a, ch, :, lanes] = value
                    buf[q, ch, a, :, lanes] = value.astype(jnp.bfloat16)

            @pl.when(n < STEPS - 1)
            def _():
                for copy in copies(q, ch):
                    copy.start()

            total = sum(fold(vecs[q, a, ch] * first[a, ch]) for a in range(2))
            at = pl.multiple_of(lax.rem(n + 1, 4) * HALF + ch * ROWS, ROWS)
            turned[(n + 1) // 4, pl.ds(at, ROWS), :] = total

        @pl.when(n == STEPS - 2)
        def _():
            for i in range(2):
                sums[0, :, i * TILE : (i + 1) * TILE] = row_of_sums(i)

        return carry

    lax.fori_loop(0, STEPS, step, 0)

    final = STEPS % 2
    give_last = pltpu.make_async_remote_copy(
        src_ref=vecs.at[final, other], dst_ref=landed, send_sem=pair_send.at[2], recv_sem=pair_recv.at[2],
        device_id=partner, device_id_type=MESH,
    )
    give_last.start()

    sums[0, :, 2 * TILE :] = row_of_sums(2)

    def share(source, gathered, me, member, steps, sent, received, meanwhile):
        partners = [member(step) for step in steps]

        def copy(i, slot):
            return pltpu.make_async_remote_copy(
                src_ref=source, dst_ref=gathered.at[slot], send_sem=sent.at[i], recv_sem=received.at[slot],
                device_id=partners[i][1], device_id_type=MESH,
            )

        for i in range(len(steps)):
            copy(i, me).start()
        gathered[me] = source[...]
        meanwhile()
        for i in range(len(steps)):
            copy(i, me).wait_send()
        for i, (who, _) in enumerate(partners):
            copy(i, who).wait_recv()
        return jnp.sum(gathered[...], axis=0)

    def assemble():
        for ch in range(CHUNKS):
            for z in range(DEPTH):
                lanes = slice(z * TILE, (z + 1) * TILE)
                mine = pl.ds(pl.multiple_of(half * HALF + ch * ROWS, ROWS), ROWS)
                last_ref[z, mine, :] = vecs[final, core, ch, :, lanes]
        for copy in (give_vecs, give_mats):
            copy.wait_send()
        for ch in range(CHUNKS):
            for copy in copies((STEPS - 1) % 2, ch):
                copy.wait_send()

    def assemble_rest():
        give_last.wait_recv()
        for ch in range(CHUNKS):
            for z in range(DEPTH):
                lanes = slice(z * TILE, (z + 1) * TILE)
                theirs = pl.ds(pl.multiple_of((1 - half) * HALF + ch * ROWS, ROWS), ROWS)
                last_ref[z, theirs, :] = landed[ch, :, lanes]
        give_last.wait_send()

    sums[1] = share(sums.at[0], gather_a, in_a, member_a, STEPS_A, a_send, a_recv, assemble)
    result_b = share(sums.at[1], gather_b, in_b, member_b, STEPS_B, b_send, b_recv, assemble_rest)
    scaled = result_b * (1.0 / (NX * NY * DEPTH * TILE))
    for n in range(STEPS + 1):
        row = jnp.broadcast_to(scaled[:, n // 4 * TILE : (n // 4 + 1) * TILE], (8, TILE))
        if n % 4:
            row = pltpu.roll(row, TILE - n % 4 * HALF, 1)
        moments_ref[n : n + 1, :] = row[0:1, :HALF]


def body(start_vecs, force_blocks, slot_offsets):
    vec_shape = (2, CHUNKS, ROWS, WIDE)
    count = len(MESSAGES)
    moments, last = pl.pallas_call(
        kernel,
        out_shape=(
            jax.ShapeDtypeStruct((STEPS + 1, HALF), jnp.float32),
            jax.ShapeDtypeStruct((DEPTH, 2 * HALF, TILE), jnp.float32),
        ),
        in_specs=[
            pl.BlockSpec(memory_space=pltpu.VMEM),
            pl.BlockSpec(memory_space=pltpu.HBM),
            pl.BlockSpec(memory_space=pltpu.HBM),
        ],
        out_specs=(pl.BlockSpec(memory_space=pltpu.VMEM), pl.BlockSpec(memory_space=pltpu.VMEM)),
        scratch_shapes=[
            pltpu.VMEM((DEPTH, 2 * HALF, TILE), jnp.float32),
            pltpu.VMEM((DEPTH * CODES, TILE, TILE), jnp.bfloat16),
            pltpu.VMEM((2, DEPTH, 27 * TILE, TILE), jnp.bfloat16),
            pltpu.VMEM((2, CHUNKS, SLOTS, ROWS, WIDE), jnp.bfloat16),
            pltpu.VMEM((2,) + vec_shape, jnp.float32),
            pltpu.VMEM(vec_shape, jnp.float32),
            pltpu.VMEM((2, CHUNKS, 1, ROWS, WIDE), jnp.bfloat16),
            pltpu.VMEM(vec_shape[1:], jnp.float32),
            pltpu.VMEM(vec_shape[1:], jnp.float32),
            pltpu.VMEM((2, 1, 3 * TILE), jnp.float32),
            pltpu.VMEM((3, TILE, TILE), jnp.float32),
            pltpu.VMEM((GROUP_A, 1, 3 * TILE), jnp.float32),
            pltpu.VMEM((GROUP_B, 1, 3 * TILE), jnp.float32),
            pltpu.SemaphoreType.DMA((2,)),
            pltpu.SemaphoreType.DMA((2, CHUNKS, count)),
            pltpu.SemaphoreType.DMA((2, CHUNKS, count)),
            pltpu.SemaphoreType.DMA((3,)),
            pltpu.SemaphoreType.DMA((3,)),
            pltpu.SemaphoreType.DMA((GROUP_A,)),
            pltpu.SemaphoreType.DMA((GROUP_A,)),
            pltpu.SemaphoreType.DMA((GROUP_B,)),
            pltpu.SemaphoreType.DMA((GROUP_B,)),
        ],
        compiler_params=pltpu.CompilerParams(
            collective_id=0, has_side_effects=True, vmem_limit_bytes=52 << 20
        ),
    )(
        slot_offsets.reshape(DEPTH, CODES),
        start_vecs.reshape(DEPTH, 2 * HALF, TILE),
        force_blocks.reshape(DEPTH * CODES, TILE, TILE),
    )
    return moments, last.reshape(1, 1, DEPTH, 2 * HALF, TILE)


def solution(mesh):
    in_specs = (
        P("gx", "gy", None, None, None),
        P("gx", "gy", None, None, None, None),
        P("gx", "gy", None, None),
    )
    out_specs = (P(), P("gx", "gy", None, None, None))
    return jax.shard_map(body, mesh=mesh, in_specs=in_specs, out_specs=out_specs, check_vma=False)
```

time: 103 us -> 98.6 us (0.957)
  Pallas kernels: 99.5 us -> 94.9 us
    pallas_call x1, Pallas kernels: 99.5 us -> 94.9 us  [body(): pl.pallas_call(kernel, out_shape=(jax.ShapeDtypeStruct((STEPS + 1, HALF),...]
    unnamed x2 -> x6, local copies, waits for them, and re-layouts: 2.86 us -> 2.83 us
where the time goes in v3:
time: 98.6 us; the launch traced here: 98.4 us
  Pallas kernels  94.9 us (96%)
  local copies, waits for them, and re-layouts  2.83 us (3%)
    pallas_call x1, Pallas kernels, body(): pl.pallas_call(kernel, out_shape=(jax.ShapeDtypeStruct((STEPS + 1, HALF),...  94.9 us
    unnamed x6, local copies, waits for them, and re-layouts  2.83 us

profile of v3, /device:TPU:1, one launch (start us, length us, event | category | flops | bytes accessed | tf_op | source)
XLA Modules:
  0.0 98.4 jit_solution(15636084655754641076)
XLA Ops:
  0.6 0.0 copy-start
  0.6 0.9 copy-done
  1.5 0.0 copy-start.1
  1.5 0.7 copy-done.1
  2.2 94.9 %shard_map.50 = (f32[9,32]{1,0:T(8,128)S(1)}, f32[4,64,128]{2,1,0:T(8,128)S(1)}) custom-call(s32[4,27]{1,0:T(4,128)S(1)} %bitcast.6, f32[4,64,128]{2,1,0:T(8,128)S(1)} %bitcast.4, bf16[108,128,128]{2,1,0:T(8,128)(2,1)} %bitcast.7), custom_call_target="tpu_custom_call" | custom-call | tf_op jit(solution)/shard_map/pallas_call | solution.py:315
  97.1 0.6 copy.7
  97.7 0.7 copy.8
Async XLA Ops:
  0.6 0.9 copy-start
  1.5 0.7 copy-start.1

commit v4 on v3

--- a/solution.py
+++ b/solution.py
@@ -30,6 +30,7 @@
 SOURCES = ((0, 1, 8, 9, 10, 11, 2, 4, 5), (0, 1, 8, 9, 10, 11, 3, 6, 7))
 PLACES = ((4, 7, 3, 6, 5, 8, 1, 0, 2), (1, 4, 0, 3, 2, 5, 7, 6, 8))
 GROUPS = (((), 0, 2), ((6, 7), 2, 6), ((0, 1, 2, 3, 4, 5), 6, 9))
+LEAVING = ((1, 4, 5, 6, 7), (0, 2, 3))
 GROUP_A, GROUP_B = 16, 32
 
 
@@ -194,61 +195,60 @@
             value = first[a, ch]
             buf[0, ch, a] = value.astype(jnp.bfloat16)
             vecs[0, a, ch] = value
-            vecs[1, a, ch] = jnp.zeros_like(value)
             total = total + fold(value * value)
         turned[0, ch * ROWS : (ch + 1) * ROWS, :] = total
     give_mats.wait_recv()
 
-    def step(n, carry):
-        p = lax.rem(n, 2)
+    def products(p, ch, a, group, accs):
+        _, begin, end = GROUPS[group]
+        pieces = [buf[p, ch, SOURCES[a][i]] for i in range(begin, end)]
+        for z in range(DEPTH):
+            low, high = window(z)
+            wide = (high - low) * TILE
+            left = jnp.concatenate([piece[:, low * TILE : high * TILE] for piece in pieces], axis=1)
+            part = jnp.dot(left, mats[a, z, begin * wide : end * wide, :], preferred_element_type=jnp.float32)
+            accs[z] = part if accs[z] is None else accs[z] + part
+
+    def step(n, p, is_first, is_last):
         q = 1 - p
-        scale = jnp.where(n == 0, 1.0, 2.0).astype(jnp.float32)
-
         for ch in range(CHUNKS):
-            accs = [[jnp.zeros((ROWS, TILE), jnp.float32) for _ in range(DEPTH)] for _ in range(2)]
+            accs = [[None] * DEPTH for _ in range(2)]
             arriving = copies(p, ch)
-            for waits, begin, end in GROUPS:
-                for i in waits:
+            for group in range(2):
+                for i in GROUPS[group][0]:
                     arriving[i].wait_recv()
                 for a in range(2):
-                    pieces = [buf[p, ch, SOURCES[a][i]] for i in range(begin, end)]
-                    for z in range(DEPTH):
-                        low, high = window(z)
-                        wide = (high - low) * TILE
-                        left = jnp.concatenate([piece[:, low * TILE : high * TILE] for piece in pieces], axis=1)
-                        accs[a][z] = accs[a][z] + jnp.dot(
-                            left, mats[a, z, begin * wide : end * wide, :], preferred_element_type=jnp.float32
-                        )
-
-            @pl.when(n >= 1)
-            def _():
+                    products(p, ch, a, group, accs[a])
+            if not is_first:
                 for copy in copies(q, ch):
                     copy.wait_send()
-
-            for a in range(2):
+            for i in GROUPS[2][0]:
+                arriving[i].wait_recv()
+            leaving = copies(q, ch)
+            for a in (1, 0):
+                products(p, ch, a, 2, accs[a])
                 for z in range(DEPTH):
                     lanes = slice(z * TILE, (z + 1) * TILE)
-                    value = scale * accs[a][z] - vecs[q, a, ch, :, lanes]
+                    value = accs[a][z] if is_first else 2.0 * accs[a][z] - vecs[q, a, ch, :, lanes]
                     vecs[q, a, ch, :, lanes] = value
-                    buf[q, ch, a, :, lanes] = value.astype(jnp.bfloat16)
-
-            @pl.when(n < STEPS - 1)
-            def _():
-                for copy in copies(q, ch):
-                    copy.start()
-
+                    if not is_last:
+                        buf[q, ch, a, :, lanes] = value.astype(jnp.bfloat16)
+                if not is_last:
+                    for i in LEAVING[a]:
+                        leaving[i].start()
             total = sum(fold(vecs[q, a, ch] * first[a, ch]) for a in range(2))
-            at = pl.multiple_of(lax.rem(n + 1, 4) * HALF + ch * ROWS, ROWS)
-            turned[(n + 1) // 4, pl.ds(at, ROWS), :] = total
-
-        @pl.when(n == STEPS - 2)
-        def _():
-            for i in range(2):
-                sums[0, :, i * TILE : (i + 1) * TILE] = row_of_sums(i)
-
+            at = lax.rem(n + 1, 4) * HALF + ch * ROWS
+            turned[(n + 1) // 4, pl.ds(pl.multiple_of(at, ROWS), ROWS), :] = total
+
+    def middle(n, carry):
+        step(n, lax.rem(n, 2), False, False)
         return carry
 
-    lax.fori_loop(0, STEPS, step, 0)
+    step(jnp.int32(0), 0, True, False)
+    lax.fori_loop(1, STEPS - 1, middle, 0)
+    for i in range(2):
+        sums[0, :, i * TILE : (i + 1) * TILE] = row_of_sums(i)
+    step(jnp.int32(STEPS - 1), (STEPS - 1) % 2, False, True)
 
     final = STEPS % 2
     give_last = pltpu.make_async_remote_copy(
@@ -349,7 +349,7 @@
             pltpu.SemaphoreType.DMA((GROUP_B,)),
         ],
         compiler_params=pltpu.CompilerParams(
-            collective_id=0, has_side_effects=True, vmem_limit_bytes=52 << 20
+            collective_id=0, has_side_effects=True, vmem_limit_bytes=55008 << 10
         ),
     )(
         slot_offsets.reshape(DEPTH, CODES),

time: 98.6 us -> 98.3 us (level)
    unnamed x6 -> x4, local copies, waits for them, and re-layouts: 2.83 us -> 1.93 us
where the time goes in v4:
time: 98.3 us; the launch traced here: 98.2 us
  Pallas kernels  95.6 us (97%)
  local copies, waits for them, and re-layouts  1.93 us (2%)
    pallas_call x1, Pallas kernels, body(): pl.pallas_call(kernel, out_shape=(jax.ShapeDtypeStruct((STEPS + 1, HALF),...  95.6 us

profile of v4, /device:TPU:1, one launch (start us, length us, event | category | flops | bytes accessed | tf_op | source)
XLA Modules:
  0.0 98.2 jit_solution(15746850721629961214)
XLA Ops:
  0.6 0.0 copy-start
  0.6 0.7 copy-done
  1.3 95.6 %shard_map.50 = (f32[9,32]{1,0:T(8,128)S(1)}, f32[4,64,128]{2,1,0:T(8,128)S(1)}) custom-call(s32[4,27]{1,0:T(4,128)S(1)} %bitcast.5, f32[4,64,128]{2,1,0:T(8,128)} %bitcast.7, bf16[108,128,128]{2,1,0:T(8,128)(2,1)} %bitcast.6), custom_call_target="tpu_custom_call" | custom-call | tf_op jit(solution)/shard_map/pallas_call | solution.py:315
  96.9 0.6 copy.7
  97.5 0.7 copy.8
Async XLA Ops:
  0.6 0.7 copy-start

commit v5 on v4

--- a/solution.py
+++ b/solution.py
@@ -30,7 +30,6 @@
 SOURCES = ((0, 1, 8, 9, 10, 11, 2, 4, 5), (0, 1, 8, 9, 10, 11, 3, 6, 7))
 PLACES = ((4, 7, 3, 6, 5, 8, 1, 0, 2), (1, 4, 0, 3, 2, 5, 7, 6, 8))
 GROUPS = (((), 0, 2), ((6, 7), 2, 6), ((0, 1, 2, 3, 4, 5), 6, 9))
-LEAVING = ((1, 4, 5, 6, 7), (0, 2, 3))
 GROUP_A, GROUP_B = 16, 32
 
 
@@ -99,7 +98,7 @@
     for step in STEPS_A:
         greet(member_a(step)[1])
 
-    turned[...] = jnp.zeros_like(turned)
+    sums[...] = jnp.zeros_like(sums)
     load_vecs.wait()
     for ch in range(CHUNKS):
         for z in range(DEPTH):
@@ -184,8 +183,8 @@
     def fold(value):
         return sum(value[:, z * TILE : (z + 1) * TILE] for z in range(DEPTH))
 
-    def row_of_sums(i):
-        return jnp.sum(jnp.transpose(turned[i]), axis=0, keepdims=True)
+    def row_of_sums(i, count):
+        return jnp.sum(jnp.transpose(turned[i, :count]), axis=0, keepdims=True)
 
     give_mats.start()
     give_vecs.wait_recv()
@@ -224,18 +223,18 @@
                     copy.wait_send()
             for i in GROUPS[2][0]:
                 arriving[i].wait_recv()
-            leaving = copies(q, ch)
-            for a in (1, 0):
+            for a in range(2):
                 products(p, ch, a, 2, accs[a])
+            for a in range(2):
                 for z in range(DEPTH):
                     lanes = slice(z * TILE, (z + 1) * TILE)
                     value = accs[a][z] if is_first else 2.0 * accs[a][z] - vecs[q, a, ch, :, lanes]
                     vecs[q, a, ch, :, lanes] = value
                     if not is_last:
                         buf[q, ch, a, :, lanes] = value.astype(jnp.bfloat16)
-                if not is_last:
-                    for i in LEAVING[a]:
-                        leaving[i].start()
+            if not is_last:
+                for copy in copies(q, ch):
+                    copy.start()
             total = sum(fold(vecs[q, a, ch] * first[a, ch]) for a in range(2))
             at = lax.rem(n + 1, 4) * HALF + ch * ROWS
             turned[(n + 1) // 4, pl.ds(pl.multiple_of(at, ROWS), ROWS), :] = total
@@ -247,7 +246,7 @@
     step(jnp.int32(0), 0, True, False)
     lax.fori_loop(1, STEPS - 1, middle, 0)
     for i in range(2):
-        sums[0, :, i * TILE : (i + 1) * TILE] = row_of_sums(i)
+        sums[0, :, i * TILE : (i + 1) * TILE] = row_of_sums(i, TILE)
     step(jnp.int32(STEPS - 1), (STEPS - 1) % 2, False, True)
 
     final = STEPS % 2
@@ -257,7 +256,7 @@
     )
     give_last.start()
 
-    sums[0, :, 2 * TILE :] = row_of_sums(2)
+    sums[0, :, 2 * TILE : 2 * TILE + HALF] = row_of_sums(2, HALF)
 
     def share(source, gathered, me, member, steps, sent, received, meanwhile):
         partners = [member(step) for step in steps]

time: 98.3 us -> 98.1 us (level)
  no operation moved by 1% of the time
where the time goes in v5:
time: 98.1 us; the launch traced here: 98 us
  Pallas kernels  95.4 us (97%)
  local copies, waits for them, and re-layouts  1.93 us (2%)
    pallas_call x1, Pallas kernels, body(): pl.pallas_call(kernel, out_shape=(jax.ShapeDtypeStruct((STEPS + 1, HALF),...  95.4 us

profile of v5, /device:TPU:1, one launch (start us, length us, event | category | flops | bytes accessed | tf_op | source)
XLA Modules:
  0.0 98.0 jit_solution(16129725993467003039)
XLA Ops:
  0.6 0.0 copy-start
  0.6 0.7 copy-done
  1.3 95.4 %shard_map.50 = (f32[9,32]{1,0:T(8,128)S(1)}, f32[4,64,128]{2,1,0:T(8,128)S(1)}) custom-call(s32[4,27]{1,0:T(4,128)S(1)} %bitcast.5, f32[4,64,128]{2,1,0:T(8,128)} %bitcast.7, bf16[108,128,128]{2,1,0:T(8,128)(2,1)} %bitcast.6), custom_call_target="tpu_custom_call" | custom-call | tf_op jit(solution)/shard_map/pallas_call | solution.py:314
  96.7 0.6 copy.7
  97.3 0.7 copy.8
Async XLA Ops:
  0.6 0.7 copy-start

commit v6 on v4

--- a/solution.py
+++ b/solution.py
@@ -52,7 +52,7 @@
 
 def kernel(
     offsets, start_hbm, blocks_hbm, moments_ref, last_ref,
-    start, blocks, mats, buf, vecs, first, own, staged, landed, sums, turned, gather_a, gather_b,
+    start, blocks, mats, buf, vecs, first, own, staged, landed, early, late, turned, early_a, early_b, late_a, late_b,
     load_sem, send, recv, pair_send, pair_recv, a_send, a_recv, b_send, b_recv,
 ):
     gx, gy = lax.axis_index("gx"), lax.axis_index("gy")
@@ -209,7 +209,29 @@
             part = jnp.dot(left, mats[a, z, begin * wide : end * wide, :], preferred_element_type=jnp.float32)
             accs[z] = part if accs[z] is None else accs[z] + part
 
-    def step(n, p, is_first, is_last):
+    def share(k, source, gathered, me, member, steps, sent, received):
+        partners = [member(step) for step in steps]
+
+        def copy(i, slot):
+            return pltpu.make_async_remote_copy(
+                src_ref=source, dst_ref=gathered.at[slot], send_sem=sent.at[k, i], recv_sem=received.at[k, slot],
+                device_id=partners[i][1], device_id_type=MESH,
+            )
+
+        for i in range(len(steps)):
+            copy(i, me).start()
+        gathered[me] = source[...]
+
+        def finish():
+            for i in range(len(steps)):
+                copy(i, me).wait_send()
+            for i, (who, _) in enumerate(partners):
+                copy(i, who).wait_recv()
+            return jnp.sum(gathered[...], axis=0)
+
+        return finish
+
+    def step(n, p, is_first, is_last, between=None):
         q = 1 - p
         for ch in range(CHUNKS):
             accs = [[None] * DEPTH for _ in range(2)]
@@ -239,6 +261,8 @@
             total = sum(fold(vecs[q, a, ch] * first[a, ch]) for a in range(2))
             at = lax.rem(n + 1, 4) * HALF + ch * ROWS
             turned[(n + 1) // 4, pl.ds(pl.multiple_of(at, ROWS), ROWS), :] = total
+            if between is not None and ch == 0:
+                between()
 
     def middle(n, carry):
         step(n, lax.rem(n, 2), False, False)
@@ -247,8 +271,15 @@
     step(jnp.int32(0), 0, True, False)
     lax.fori_loop(1, STEPS - 1, middle, 0)
     for i in range(2):
-        sums[0, :, i * TILE : (i + 1) * TILE] = row_of_sums(i)
-    step(jnp.int32(STEPS - 1), (STEPS - 1) % 2, False, True)
+        early[0, :, i * TILE : (i + 1) * TILE] = row_of_sums(i)
+    finish_early_a = share(0, early.at[0], early_a, in_a, member_a, STEPS_A, a_send, a_recv)
+    finish_early = []
+
+    def between():
+        early[1] = finish_early_a()
+        finish_early.append(share(0, early.at[1], early_b, in_b, member_b, STEPS_B, b_send, b_recv))
+
+    step(jnp.int32(STEPS - 1), (STEPS - 1) % 2, False, True, between)
 
     final = STEPS % 2
     give_last = pltpu.make_async_remote_copy(
@@ -257,26 +288,7 @@
     )
     give_last.start()
 
-    sums[0, :, 2 * TILE :] = row_of_sums(2)
-
-    def share(source, gathered, me, member, steps, sent, received, meanwhile):
-        partners = [member(step) for step in steps]
-
-        def copy(i, slot):
-            return pltpu.make_async_remote_copy(
-                src_ref=source, dst_ref=gathered.at[slot], send_sem=sent.at[i], recv_sem=received.at[slot],
-                device_id=partners[i][1], device_id_type=MESH,
-            )
-
-        for i in range(len(steps)):
-            copy(i, me).start()
-        gathered[me] = source[...]
-        meanwhile()
-        for i in range(len(steps)):
-            copy(i, me).wait_send()
-        for i, (who, _) in enumerate(partners):
-            copy(i, who).wait_recv()
-        return jnp.sum(gathered[...], axis=0)
+    late[0] = row_of_sums(2)
 
     def assemble():
         for ch in range(CHUNKS):
@@ -299,8 +311,12 @@
                 last_ref[z, theirs, :] = landed[ch, :, lanes]
         give_last.wait_send()
 
-    sums[1] = share(sums.at[0], gather_a, in_a, member_a, STEPS_A, a_send, a_recv, assemble)
-    result_b = share(sums.at[1], gather_b, in_b, member_b, STEPS_B, b_send, b_recv, assemble_rest)
+    finish_late_a = share(1, late.at[0], late_a, in_a, member_a, STEPS_A, a_send, a_recv)
+    assemble()
+    late[1] = finish_late_a()
+    finish_late_b = share(1, late.at[1], late_b, in_b, member_b, STEPS_B, b_send, b_recv)
+    assemble_rest()
+    result_b = jnp.concatenate([finish_early[0](), finish_late_b()], axis=1)
     scaled = result_b * (1.0 / (NX * NY * DEPTH * TILE))
     for n in range(STEPS + 1):
         row = jnp.broadcast_to(scaled[:, n // 4 * TILE : (n // 4 + 1) * TILE], (8, TILE))
@@ -334,19 +350,22 @@
             pltpu.VMEM((2, CHUNKS, 1, ROWS, WIDE), jnp.bfloat16),
             pltpu.VMEM(vec_shape[1:], jnp.float32),
             pltpu.VMEM(vec_shape[1:], jnp.float32),
-            pltpu.VMEM((2, 1, 3 * TILE), jnp.float32),
+            pltpu.VMEM((2, 1, 2 * TILE), jnp.float32),
+            pltpu.VMEM((2, 1, TILE), jnp.float32),
             pltpu.VMEM((3, TILE, TILE), jnp.float32),
-            pltpu.VMEM((GROUP_A, 1, 3 * TILE), jnp.float32),
-            pltpu.VMEM((GROUP_B, 1, 3 * TILE), jnp.float32),
+            pltpu.VMEM((GROUP_A, 1, 2 * TILE), jnp.float32),
+            pltpu.VMEM((GROUP_B, 1, 2 * TILE), jnp.float32),
+            pltpu.VMEM((GROUP_A, 1, TILE), jnp.float32),
+            pltpu.VMEM((GROUP_B, 1, TILE), jnp.float32),
             pltpu.SemaphoreType.DMA((2,)),
             pltpu.SemaphoreType.DMA((2, CHUNKS, count)),
             pltpu.SemaphoreType.DMA((2, CHUNKS, count)),
             pltpu.SemaphoreType.DMA((3,)),
             pltpu.SemaphoreType.DMA((3,)),
-            pltpu.SemaphoreType.DMA((GROUP_A,)),
-            pltpu.SemaphoreType.DMA((GROUP_A,)),
-            pltpu.SemaphoreType.DMA((GROUP_B,)),
-            pltpu.SemaphoreType.DMA((GROUP_B,)),
+            pltpu.SemaphoreType.DMA((2, GROUP_A)),
+            pltpu.SemaphoreType.DMA((2, GROUP_A)),
+            pltpu.SemaphoreType.DMA((2, GROUP_B)),
+            pltpu.SemaphoreType.DMA((2, GROUP_B)),
         ],
         compiler_params=pltpu.CompilerParams(
             collective_id=0, has_side_effects=True, vmem_limit_bytes=55008 << 10

time: 98.3 us -> 99.2 us (level)
  no operation moved by 1% of the time
where the time goes in v6:
time: 99.2 us; the launch traced here: 99 us
  Pallas kernels  96.4 us (97%)
  local copies, waits for them, and re-layouts  1.93 us (2%)
    pallas_call x1, Pallas kernels, body(): pl.pallas_call(kernel, out_shape=(jax.ShapeDtypeStruct((STEPS + 1, HALF),...  96.4 us

profile of v6, /device:TPU:1, one launch (start us, length us, event | category | flops | bytes accessed | tf_op | source)
XLA Modules:
  0.0 99.0 jit_solution(10951903569183442988)
XLA Ops:
  0.6 0.0 copy-start
  0.6 0.7 copy-done
  1.3 96.4 %shard_map.50 = (f32[9,32]{1,0:T(8,128)S(1)}, f32[4,64,128]{2,1,0:T(8,128)S(1)}) custom-call(s32[4,27]{1,0:T(4,128)S(1)} %bitcast.5, f32[4,64,128]{2,1,0:T(8,128)} %bitcast.7, bf16[108,128,128]{2,1,0:T(8,128)(2,1)} %bitcast.6), custom_call_target="tpu_custom_call" | custom-call | tf_op jit(solution)/shard_map/pallas_call | solution.py:331
  97.8 0.6 copy.7
  98.4 0.7 copy.8
Async XLA Ops:
  0.6 0.7 copy-start
